TPU v7x, 32 devices: a whole 2x2x4 slice. The times are simulated.
32 devices in a mesh: grp: 2 (over y), side: 4 (over z), shard: 4 (over x, core).
Axes of the slice: x: 2, y: 2, z: 4, core: 2. Of those that a mesh axis runs over, the one named last changes fastest.
Arguments:
- queries: bfloat16 [480, 8192], P(('grp', 'side', 'shard')), parts along dimension 0, may hold values from -6.5 to 6.5
- new_kv: bfloat16 [480, 2048], P(('grp', 'side', 'shard')), parts along dimension 0, may hold values from -4.5 to 4.5
- kv_pool: bfloat16 [3584, 16, 2048], P(('grp', 'side', 'shard')), parts along dimension 0, may hold values from -4.5 to 4.5
- page_table: int32 [480, 16], P(('grp', 'side', 'shard')), parts along dimension 0, may hold values from 0 to 111, as said below
- ctx_len: int32 [480], P(('grp', 'side', 'shard')), parts along dimension 0, may hold values from 0 to 256, as said below
- residual_in: bfloat16 [480, 8192], P(('grp', 'side', 'shard')), parts along dimension 0, may hold values from -6 to 6
- norm_gain: bfloat16 [8192], replicated, may hold values from 0.5 to 1.5
- w_up: bfloat16 [8192, 16384], P('side', 'shard'), may hold values from -0.0625 to 0.0625
- w_down: bfloat16 [16384, 8192], P('shard', 'side'), may hold values from -0.046875 to 0.046875
Outputs:
- layer_out: bfloat16 [480, 8192], P(('grp', 'side', 'shard')), parts along dimension 0
There are 2 independent parts, one for each index of `grp`. A program takes and returns all parts, laid end to end along the dimension named above; an argument that names none is the same for every part. Nothing has to cross between parts.
Inputs may be any that keep to these rules, and one draw needn't show every extreme that they name: `ctx_len`: on one device's 15 slots, 3 to 12 have a nonzero length, exactly 12 on some device; a live slot's pages together hold at most 112 pages on its device; every device has a slot of length 256. `page_table`: the first ceil(ctx_len / 16) entries of a live slot name distinct pages, and no page is named by two live slots of one device; other entries name valid pages.
All inputs are finite; a program needn't handle non-finite values.
Results may differ from a plain program's by a relative error of at most 0.009.
Values may be sent and summed in bfloat16 or wider, within the bound.
No kernel may reach another device: no remote copies, remote signals or barrier semaphores. Data moves between devices by JAX's collectives and lax.ppermute only.
A program may use at most 128 MiB of HBM per device.

v0:
```python
import math

import jax
import jax.numpy as jnp
from jax import lax
from jax.sharding import PartitionSpec as P

KV_HEADS = 8
HEAD = 128
GROUP = 8


epsilon = 1e-05


def attend_slots(queries, new_kv, pool_pages, page_rows, lengths):
    slot_count = queries.shape[0]
    positions = page_rows.shape[1] * pool_pages.shape[1]
    fetched = pool_pages[page_rows].reshape(slot_count, positions, 2, KV_HEADS, HEAD)
    fresh_kv = new_kv.reshape(slot_count, 2, KV_HEADS, HEAD)
    query_heads = queries.reshape(slot_count, KV_HEADS, GROUP, HEAD)
    score_scale = 1.0 / math.sqrt(HEAD)
    scores = (
        jnp.einsum(
            "sgqd,slgd->sgql", query_heads, fetched[:, :, 0], preferred_element_type=jnp.float32
        )
        * score_scale
    )
    own_score = (
        jnp.einsum("sgqd,sgd->sgq", query_heads, fresh_kv[:, 0], preferred_element_type=jnp.float32)
        * score_scale
    )
    visible = (jnp.arange(positions, dtype=jnp.int32)[None, :] < lengths[:, None])[:, None, None, :]
    scores = jnp.where(visible, scores, -1e30)
    highest = jnp.maximum(jnp.max(scores, axis=-1), own_score)
    weights = jnp.where(visible, jnp.exp(scores - highest[..., None]), 0.0)
    own_weight = jnp.exp(own_score - highest)
    denominator = jnp.sum(weights, axis=-1) + own_weight
    probabilities = (weights / denominator[..., None]).astype(jnp.bfloat16)
    own_prob = (own_weight / denominator).astype(jnp.bfloat16).astype(jnp.float32)
    attended = jnp.einsum(
        "sgql,slgd->sgqd", probabilities, fetched[:, :, 1], preferred_element_type=jnp.float32
    )
    attended = attended + own_prob[..., None] * fresh_kv[:, 1].astype(jnp.float32)[:, :, None, :]
    return attended.reshape(slot_count, -1)


def shards(queries, new_kv, kv_pool, page_table, ctx_len, residual_in, norm_gain, w_up, w_down):
    attended = attend_slots(queries, new_kv, kv_pool, page_table, ctx_len)
    mixed_rows = residual_in.astype(jnp.float32) + attended
    mean_square = jnp.mean(mixed_rows * mixed_rows, axis=-1, keepdims=True)
    normed = (mixed_rows * lax.rsqrt(mean_square + epsilon) * norm_gain.astype(jnp.float32)).astype(
        jnp.bfloat16
    )
    live_mask = ctx_len > 0
    spread = lax.all_to_all(normed, "side", split_axis=1, concat_axis=0, tiled=True)
    up_partial = jnp.dot(
        lax.all_gather(spread, "shard", axis=0, tiled=True),
        w_up,
        preferred_element_type=jnp.float32,
    )
    lifted = lax.psum(up_partial, "side")
    clipped = jnp.maximum(lifted, 0.0)
    active = (clipped * clipped).astype(jnp.bfloat16)
    down_share = lax.psum_scatter(
        jnp.dot(active, w_down, preferred_element_type=jnp.float32).astype(jnp.bfloat16),
        "shard",
        scatter_dimension=0,
        tiled=True,
    ).astype(jnp.float32)
    returned = lax.all_to_all(
        down_share.astype(jnp.bfloat16), "side", split_axis=0, concat_axis=1, tiled=True
    ).astype(down_share.dtype)
    returned = jnp.where(live_mask[:, None], returned, 0.0)
    return (mixed_rows + returned).astype(jnp.bfloat16)


def solution(mesh):
    placed = (
        P(("grp", "side", "shard"), None),
        P(("grp", "side", "shard"), None),
        P(("grp", "side", "shard"), None, None),
        P(("grp", "side", "shard"), None),
        P(("grp", "side", "shard")),
        P(("grp", "side", "shard"), None),
        P(),
        P("side", "shard"),
        P("shard", "side"),
    )
    return jax.shard_map(
        shards,
        mesh=mesh,
        in_specs=placed,
        out_specs=P(("grp", "side", "shard"), None),
        check_vma=False,
    )
```

profile of v0, /device:TPU:0, one launch (start us, length us, event | category | flops | bytes accessed | tf_op | source)
XLA Modules:
  0.0 268.1 jit_solution(1163020549777646393)
XLA Ops:
  6.5 0.0 all-reduce.4.cloned.1.call-start
  6.5 0.7 iota_compare_fusion
  7.3 0.7 compare_select_fusion
  8.0 0.1 reshape.65
  8.1 12.4 %gather_fusion = bf16[240,16,2048]{2,1,0:T(8,128)(2,1)} fusion(bf16[112,16,2048]{2,1,0:T(8,128)(2,1)} %param.11, s32[1024]{0:T(1024)S(1)} %pad_clamp_fusion), kind=kCustom, calls=%fused_computation | custom fusion | bytes 31458240 | tf_op jit(solution)/shard_map/gather | solution.py:19
  20.5 9.3 %copy.31 = bf16[480,8,16,128]{3,2,1,0:T(8,128)(2,1)S(1)} copy(bf16[480,8,16,128]{3,1,2,0:T(8,128)(2,1)} %bitcast.69) | data formatting | bytes 31457280
  29.7 0.0 copy-start.1
  29.7 0.0 copy-start.2
  29.8 2.9 %fusion.25 = (bf16[15,256,1,8,128]{4,3,2,1,0:T(8,128)(2,1)S(1)}, bf16[15,256,1,8,128]{4,3,2,1,0:T(8,128)(2,1)S(1)}) fusion(bf16[15,256,2,8,128]{4,3,2,1,0:T(8,128)(2,1)S(1)} %bitcast.68), kind=kLoop, calls=%fused_computation.48 | loop fusion | bytes 31457280 | tf_op jit(solution)/shard_map/slice | solution.py:25
  32.6 0.0 copy-done.1
  32.7 0.0 copy-done.2
  32.7 0.3 fusion.14
  33.0 2.2 fusion.26
  35.3 0.4 fusion.9
  35.7 0.0 copy-start
  35.7 0.0 copy-start.3
  35.7 1.2 fusion.8
  37.0 0.1 pad.2
  37.0 0.3 copy.34
  37.3 0.0 copy-done
  37.3 0.2 multiply_reduce_fusion
  37.6 0.1 multiply_convert_fusion.2
  37.7 0.2 all_to_all.24
  37.9 0.1 copy.24
  38.1 15.2 %all_to_all.32 = bf16[15,4,2048]{2,0,1:T(8,128)(2,1)S(1)} all-to-all(bf16[15,4,2048]{2,0,1:T(8,128)(2,1)S(1)} %copy.24), channel_id=1, replica_groups=mesh['grp'=2,'side'=4,'shard'=4] {'side'}, dimensions={1} | all-to-all | bytes 491520 | tf_op jit(solution)/shard_map/all_to_all | solution.py:56
  53.3 0.1 reshape.74
  53.4 9.8 %all-gather = bf16[4,60,2048]{2,1,0:T(8,128)(2,1)S(1)} all-gather(bf16[1,60,2048]{2,1,0:T(8,128)(2,1)S(1)} %reshape.74), channel_id=1, replica_groups=mesh['grp'=2,'side'=4,'shard'=4] {'shard'}, dimensions={0}, use_global_device_ids=true | all-gather | bytes 1228800 | tf_op jit(solution)/shard_map/all_gather | solution.py:58
  63.2 0.2 reshape.75
  63.4 9.9 %fusion.27 = f32[240,4096]{1,0:T(8,128)} fusion(bf16[240,2048]{1,0:T(8,128)(2,1)S(1)} %reshape.75, bf16[2048,4096]{1,0:T(8,128)(2,1)} %param.16), kind=kOutput, calls=%fused_computation.50 | convolution fusion | flops 4026531840 | bytes 21692416 | tf_op jit(solution)/shard_map/dot_general | solution.py:57
  73.3 0.0 all-reduce.4.cloned.1.call-update
  73.3 0.0 copy-start.5
  73.3 0.0 copy-start.4
  73.3 145.0 %all-reduce.4.cloned.1.call-done = f32[240,4096]{1,0:T(8,128)} async-done(((f32[240,4096]{1,0:T(8,128)}), f32[240,4096]{1,0:T(8,128)}) %all-reduce.4.cloned.1.call-update) | async-done | bytes 3932176 | tf_op jit(solution)/shard_map/psum | solution.py:62
  218.4 11.2 %convolution_convert_fusion = bf16[240,2048]{1,0:T(8,128)(2,1)S(1)} fusion(bf16[4096,2048]{1,0:T(8,128)(2,1)} %param.17, f32[240,4096]{1,0:T(8,128)} %all-reduce.4.cloned.1.call-done), kind=kOutput, calls=%fused_computation.6 | convolution fusion | flops 4029972480 | bytes 21692416 | tf_op jit(solution)/shard_map/dot_general | solution.py:66
  229.6 14.4 %fusion = bf16[64,2048]{1,0:T(8,128)(2,1)S(1)} fusion(bf16[240,2048]{1,0:T(8,128)(2,1)S(1)} %convolution_convert_fusion), kind=kCustom, calls=%all-reduce-scatter | all-reduce-scatter fusion | flops 524289 | bytes 1245696
  243.9 1.3 collective-permute-start
  245.3 0.6 dynamic-slice.4
  246.5 0.0 collective-permute-done
  246.5 0.3 concatenate
  246.8 0.1 constant_dynamic-slice_fusion
  246.9 0.8 all_to_all.28
  247.7 3.4 %all-to-all-start.1 = ((bf16[4,15,2048]{2,1,0:T(8,128)(2,1)}), bf16[4,15,2048]{2,1,0:T(8,128)(2,1)S(1)}, u32[]{:S(2)}, u32[]{:S(2)}) async-start(bf16[4,15,2048]{2,1,0:T(8,128)(2,1)} %all_to_all.28), calls=%async_computation.1 | async-start | bytes 524288 | tf_op jit(solution)/shard_map/all_to_all | solution.py:71
  251.1 0.0 copy-done.4
  251.1 8.5 %all-to-all-done.1 = bf16[4,15,2048]{2,1,0:T(8,128)(2,1)S(1)} async-done(((bf16[4,15,2048]{2,1,0:T(8,128)(2,1)}), bf16[4,15,2048]{2,1,0:T(8,128)(2,1)S(1)}, u32[]{:S(2)}, u32[]{:S(2)}) %all-to-all-start.1) | async-done | bytes 245792 | tf_op jit(solution)/shard_map/all_to_all | solution.py:71
  259.7 0.3 copy.25
  260.0 0.1 pad.3
  260.1 0.3 copy.35
  260.5 0.8 add_convert_fusion
  (14 shorter events, 0.2 us)
Async XLA Ops:
  6.5 211.8 %all-reduce.4.cloned.1.call-start = ((), (), s32[]{:S(2)}) async-start(), calls=%async_computation.2 | async-start | bytes 7864320 | tf_op jit(solution)/shard_map/psum | solution.py:62
  29.7 2.9 %copy-start.1 = (bf16[15,8192]{1,0:T(8,128)(2,1)S(1)}, bf16[15,8192]{1,0:T(8,128)(2,1)}, u32[]{:S(2)}) copy-start(bf16[15,8192]{1,0:T(8,128)(2,1)} %param.9) | copy-start | bytes 737284
  29.7 2.9 %copy-start.2 = (bf16[15,2048]{1,0:T(8,128)(2,1)S(1)}, bf16[15,2048]{1,0:T(8,128)(2,1)}, u32[]{:S(2)}) copy-start(bf16[15,2048]{1,0:T(8,128)(2,1)} %param.10) | copy-start | bytes 184324
  35.7 1.7 copy-start
  35.7 1.9 copy-start.3
  73.3 171.9 %copy-start.5 = (u32[32]{0:T(128)S(1)}, u32[32]{0:T(128)}, u32[]{:S(2)}) copy-start(u32[32]{0:T(128)} %constant.28) | copy-start | bytes 388
  73.3 177.8 %copy-start.4 = (s32[15]{0:T(128)S(1)}, s32[15]{0:T(128)}, u32[]{:S(2)}) copy-start(s32[15]{0:T(128)} %param.13) | copy-start | bytes 184
  243.9 2.6 collective-permute-start
  247.7 12.0 %all-to-all-start.1 = ((bf16[4,15,2048]{2,1,0:T(8,128)(2,1)}), bf16[4,15,2048]{2,1,0:T(8,128)(2,1)S(1)}, u32[]{:S(2)}, u32[]{:S(2)}) async-start(bf16[4,15,2048]{2,1,0:T(8,128)(2,1)} %all_to_all.28), calls=%async_computation.1 | async-start | bytes 524288 | tf_op jit(solution)/shard_map/all_to_all | solution.py:71
Sparse Core Ops, SparseCore 0:
  73.4 144.8 all-reduce.3
where the time goes:
time: 270 us; the launch traced here: 268 us
  waiting for transfers between devices  154 us (57%)
  blocking collectives  39.4 us (15%)
  local copies, waits for them, and re-layouts  28.2 us (10%)
  matrix products  24.8 us (9%)
  between operations  14.4 us (5%)
  starting transfers between devices  4.7 us (2%)
  other arithmetic  3.09 us (1%)
    psum x1, waiting for transfers between devices, shards(): lifted = lax.psum(up_partial, 'side')  145 us
    all_to_all x1, blocking collectives, shards(): lax.all_to_all(normed, 'side', split_axis=1, concat_axis=0, tiled=True)  15.2 us
    unnamed x1, blocking collectives  14.4 us
    gather x1, local copies, waits for them, and re-layouts, attend_slots(): pool_pages[page_rows].reshape(slot_count, positions, 2, KV_HEADS, HEAD)  12.4 us
    unnamed x25, local copies, waits for them, and re-layouts  11.4 us
    dot_general x1, matrix products, shards(): jnp.dot(active, w_down, preferred_element_type=jnp.float32)  11.2 us
    dot_general x1, matrix products, shards(): jnp.dot(lax.all_gather(spread, 'shard', axis=0, tiled=True), w_up, prefer...  9.92 us
    all_gather x1, blocking collectives, shards(): lax.all_gather(spread, 'shard', axis=0, tiled=True)  9.79 us
  transfers between devices with their start and end apart: 3, of which 2 were waited for; matrix products, arithmetic and copies ran while one was open for 0% of the time, Pallas kernels for 0%

commit v1 on v0

v1 whole, which is shorter than its diff:
```python
import functools
import math

import jax
import jax.numpy as jnp
from jax import lax
from jax.experimental import pallas as pl
from jax.experimental.pallas import tpu as pltpu
from jax.sharding import PartitionSpec as P

KV_HEADS = 8
HEAD = 128
GROUP = 8
LIVE_CAP = 12
PAD = 16

epsilon = 1e-05
bf16, f32, i32 = jnp.bfloat16, jnp.float32, jnp.int32
VMEM_MB = 1 << 20


def params(mb, **more):
    return pltpu.CompilerParams(vmem_limit_bytes=mb * VMEM_MB, **more)


def cost(flops, bytes_accessed):
    return pl.CostEstimate(flops=int(flops), bytes_accessed=int(bytes_accessed), transcendentals=0)


def pad_rows(x):
    rows = x.shape[0]
    if rows == PAD:
        return x
    return jnp.concatenate([x, jnp.zeros((PAD - rows,) + x.shape[1:], x.dtype)], axis=0)


def live_ranks(lengths, slots):
    live, rank, count = [], [], jnp.int32(0)
    for slot in range(slots):
        alive = lengths[slot] > 0
        live.append(alive)
        rank.append(count)
        count = count + alive.astype(i32)
    return live, rank


def attend_kernel(
    lengths, where_side, q_ref, nk_ref, nv_ref, k_ref, v_ref, table_ref, res_ref, gain_ref, *rest
):
    sides = len(rest) - 3
    mixed_ref, sends, bias_ref, square_ref = rest[0], rest[1 : 1 + sides], rest[-2], rest[-1]
    head = pl.program_id(0)
    slots = q_ref.shape[0]
    pages, page = k_ref.shape[0], k_ref.shape[1]
    tokens = pages * page
    width = mixed_ref.shape[1]
    scale = math.log2(math.e) / math.sqrt(HEAD)

    @pl.when(head == 0)
    def _():
        lanes = 128 * ((pages + 127) // 128)
        row = lax.broadcasted_iota(i32, (PAD, lanes), 0)
        column = lax.broadcasted_iota(i32, (PAD, lanes), 1)
        reach = jnp.zeros((PAD, lanes), i32)
        for slot in range(slots):
            reach = jnp.where(row == slot, lengths[slot], reach)
        table = pad_rows(table_ref[...])
        seen = jnp.zeros((PAD, lanes), i32)
        for entry in range(table.shape[1]):
            here = jnp.minimum(jnp.maximum(reach - entry * page, 0), page)
            seen = seen + jnp.where(table[:, entry : entry + 1] == column, here, 0)
        spread = (
            lax.broadcasted_iota(i32, (lanes, tokens), 1) // page
            == lax.broadcasted_iota(i32, (lanes, tokens), 0)
        )
        seen_tokens = jnp.dot(
            seen.astype(f32).astype(bf16),
            spread.astype(f32).astype(bf16),
            preferred_element_type=f32,
        )
        place = (lax.broadcasted_iota(i32, (PAD, tokens), 1) % page).astype(f32)
        bias_ref[...] = jnp.where(place < seen_tokens, 0.0, -1e30)
        square_ref[...] = jnp.zeros_like(square_ref)

    q = jnp.concatenate(
        [pad_rows(q_ref[:, g * HEAD : (g + 1) * HEAD]) for g in range(GROUP)], axis=0
    )
    keys = k_ref[...].reshape(tokens, HEAD)
    values = v_ref[...].reshape(tokens, HEAD)
    new_key = pad_rows(nk_ref[...]).astype(f32)
    new_value = pad_rows(nv_ref[...]).astype(f32)
    scores = lax.dot_general(q, keys, (((1,), (1,)), ((), ())), preferred_element_type=f32)
    scores = scores.reshape(GROUP, PAD, tokens) * scale + bias_ref[...][None]
    own = jnp.sum(q.astype(f32).reshape(GROUP, PAD, HEAD) * new_key[None], axis=-1, keepdims=True)
    own = own * scale
    highest = jnp.maximum(jnp.max(scores, axis=-1, keepdims=True), own)
    weights = jnp.exp2(scores - highest)
    own_weight = jnp.exp2(own - highest)
    total = jnp.sum(weights, axis=-1, keepdims=True) + own_weight
    summed = jnp.dot(
        weights.astype(bf16).reshape(GROUP * PAD, tokens), values, preferred_element_type=f32
    ).reshape(GROUP, PAD, HEAD)
    attended = (summed + own_weight * new_value[None]) / total
    squares = jnp.zeros((slots, HEAD), f32)
    base = pl.multiple_of(head * (GROUP * HEAD), GROUP * HEAD)
    for g in range(GROUP):
        mixed = res_ref[:, g * HEAD : (g + 1) * HEAD].astype(f32) + attended[g][:slots]
        mixed_ref[:, pl.ds(base + g * HEAD, HEAD)] = mixed
        squares = squares + mixed * mixed
    square_ref[...] += squares

    @pl.when(head == KV_HEADS - 1)
    def _():
        live, rank = live_ranks(lengths, slots)
        row = lax.broadcasted_iota(i32, (PAD, PAD), 0)
        column = lax.broadcasted_iota(i32, (PAD, PAD), 1)
        pick = jnp.zeros((PAD, PAD), f32)
        for slot in range(slots):
            chosen = jnp.logical_and(row == rank[slot], column == slot)
            pick = jnp.where(jnp.logical_and(chosen, live[slot]), 1.0, pick)
        pick = pick.astype(bf16)
        root = lax.rsqrt(jnp.sum(square_ref[...], axis=-1, keepdims=True) / width + epsilon)
        step = width // sides
        for shift in range(sides):
            at = pl.multiple_of(lax.rem(where_side[0] + shift, sides) * step, step)
            normed = mixed_ref[:, pl.ds(at, step)] * root * gain_ref[:, pl.ds(at, step)].astype(f32)
            normed = pad_rows(normed.astype(bf16))
            sends[shift][...] = jnp.dot(pick, normed, preferred_element_type=f32).astype(bf16)


def attend(queries, new_kv, kv_pool, page_table, ctx_len, residual_in, norm_gain, side, sides):
    slots, width = queries.shape
    pages, page, _ = kv_pool.shape
    tokens = pages * page
    step = width // sides
    head_block = lambda g, *_: (0, g)
    fixed = lambda g, *_: (0, 0)
    return pl.pallas_call(
        attend_kernel,
        grid_spec=pltpu.PrefetchScalarGridSpec(
            num_scalar_prefetch=2,
            grid=(KV_HEADS,),
            in_specs=[
                pl.BlockSpec((slots, GROUP * HEAD), head_block),
                pl.BlockSpec((slots, HEAD), head_block),
                pl.BlockSpec((slots, HEAD), lambda g, *_: (0, KV_HEADS + g)),
                pl.BlockSpec((pages, page, HEAD), lambda g, *_: (0, 0, g)),
                pl.BlockSpec((pages, page, HEAD), lambda g, *_: (0, 0, KV_HEADS + g)),
                pl.BlockSpec(page_table.shape, fixed),
                pl.BlockSpec((slots, GROUP * HEAD), head_block),
                pl.BlockSpec((1, width), fixed),
            ],
            out_specs=[pl.BlockSpec((slots, width), fixed)]
            + [pl.BlockSpec((PAD, step), fixed)] * sides,
            scratch_shapes=[pltpu.VMEM((PAD, tokens), f32), pltpu.VMEM((slots, HEAD), f32)],
        ),
        out_shape=[jax.ShapeDtypeStruct((slots, width), f32)]
        + [jax.ShapeDtypeStruct((PAD, step), bf16)] * sides,
        compiler_params=params(24),
        cost_estimate=cost(4 * 8 * 128 * 128 * tokens, kv_pool.size * 2),
        name="attend",
    )(
        ctx_len, side, queries, new_kv, new_kv, kv_pool, kv_pool, page_table, residual_in,
        norm_gain.reshape(1, width),
    )


def pack_up_kernel(meta, *refs, parts):
    gathered, w_ref, packed_ref, out_ref = refs[:parts], refs[parts], refs[-2], refs[-1]
    rows = packed_ref.shape[0]

    @pl.when(pl.program_id(0) == 0)
    def _():
        per = gathered[0].shape[0]
        pieces = per // PAD
        total = jnp.zeros(packed_ref.shape, f32)
        for part in range(parts):
            lane = lax.broadcasted_iota(i32, (rows, per), 1)
            row = lax.broadcasted_iota(i32, (rows, per), 0)
            target = jnp.full((rows, per), -1, i32)
            for piece in range(pieces):
                base = meta[1 + part * pieces + piece]
                count = meta[1 + parts * pieces + part * pieces + piece]
                inside = lane - piece * PAD
                mine = jnp.logical_and(inside >= 0, inside < count)
                target = jnp.where(mine, base + inside, target)
            pick = (target == row).astype(f32).astype(bf16)
            total = total + jnp.dot(pick, gathered[part][...], preferred_element_type=f32)
        packed_ref[...] = total.astype(bf16)

    out_ref[...] = jnp.dot(packed_ref[...], w_ref[...], preferred_element_type=f32).astype(out_ref.dtype)


def up_kernel(meta, x_ref, w_ref, out_ref):
    out_ref[...] = jnp.dot(x_ref[...], w_ref[...], preferred_element_type=f32).astype(out_ref.dtype)


TILE = 256


def pack_up(meta, gathered, w_up, rows, block_width):
    depth = w_up.shape[0]
    tiles = block_width // TILE
    fixed = lambda t, *_: (0, 0)
    return pl.pallas_call(
        functools.partial(pack_up_kernel, parts=len(gathered)),
        grid_spec=pltpu.PrefetchScalarGridSpec(
            num_scalar_prefetch=1,
            grid=(tiles,),
            in_specs=[pl.BlockSpec(g.shape, fixed) for g in gathered]
            + [pl.BlockSpec((depth, TILE), lambda t, meta: (0, meta[0] * tiles + t))],
            out_specs=[
                pl.BlockSpec((rows, depth), fixed),
                pl.BlockSpec((rows, TILE), lambda t, *_: (0, t)),
            ],
        ),
        out_shape=[
            jax.ShapeDtypeStruct((rows, depth), bf16),
            jax.ShapeDtypeStruct((rows, block_width), bf16),
        ],
        compiler_params=params(24),
        cost_estimate=cost(2 * rows * depth * block_width, depth * block_width * 2),
        name="pack_up",
    )(meta, *gathered, w_up)


def up(meta, packed, w_up, block_width, dtype):
    rows, depth = packed.shape
    tiles = block_width // TILE
    return pl.pallas_call(
        up_kernel,
        grid_spec=pltpu.PrefetchScalarGridSpec(
            num_scalar_prefetch=1,
            grid=(tiles,),
            in_specs=[
                pl.BlockSpec((rows, depth), lambda t, *_: (0, 0)),
                pl.BlockSpec((depth, TILE), lambda t, meta: (0, meta[0] * tiles + t)),
            ],
            out_specs=pl.BlockSpec((rows, TILE), lambda t, *_: (0, t)),
        ),
        out_shape=jax.ShapeDtypeStruct((rows, block_width), dtype),
        compiler_params=params(16),
        cost_estimate=cost(2 * rows * depth * block_width, depth * block_width * 2),
        name="up",
    )(meta, packed, w_up)


def down_kernel(meta, *refs, first):
    a_ref, w_ref = refs[0], refs[1]
    out_ref = refs[-1]
    part = jnp.dot(a_ref[...], w_ref[...], preferred_element_type=f32)
    out_ref[...] = part if first else refs[2][...] + part


def down(meta, active, w_down, before):
    rows, depth = active.shape
    width = w_down.shape[1]
    tile = 512
    sums = pl.BlockSpec((rows, tile), lambda t, *_: (0, t))
    return pl.pallas_call(
        functools.partial(down_kernel, first=before is None),
        grid_spec=pltpu.PrefetchScalarGridSpec(
            num_scalar_prefetch=1,
            grid=(width // tile,),
            in_specs=[
                pl.BlockSpec((rows, depth), lambda t, *_: (0, 0)),
                pl.BlockSpec((depth, tile), lambda t, meta: (meta[0], t)),
            ]
            + ([] if before is None else [sums]),
            out_specs=sums,
        ),
        out_shape=jax.ShapeDtypeStruct((rows, width), f32),
        compiler_params=params(16),
        cost_estimate=cost(2 * rows * depth * width, depth * width * 2),
        name="down",
    )(meta, active, w_down, *([] if before is None else [before]))


def down_unpack_kernel(meta, a_ref, w_ref, before_ref, *outs):
    parts = len(outs)
    rows = a_ref.shape[0]
    pieces = outs[0].shape[0] // PAD
    share = before_ref[...] + jnp.dot(a_ref[...], w_ref[...], preferred_element_type=f32)
    share = share.astype(bf16)
    row = lax.broadcasted_iota(i32, (PAD, rows), 0)
    column = lax.broadcasted_iota(i32, (PAD, rows), 1)
    for part in range(parts):
        picks = []
        for piece in range(pieces):
            base = meta[1 + part * pieces + piece]
            count = meta[1 + parts * pieces + part * pieces + piece]
            picks.append(jnp.logical_and(column - row == base, row < count).astype(f32))
        pick = jnp.concatenate(picks, axis=0).astype(bf16)
        outs[part][...] = jnp.dot(pick, share, preferred_element_type=f32).astype(bf16)


def down_unpack(meta, active, w_down, before, parts, per):
    rows, depth = active.shape
    width = w_down.shape[1]
    tile = 512
    return pl.pallas_call(
        down_unpack_kernel,
        grid_spec=pltpu.PrefetchScalarGridSpec(
            num_scalar_prefetch=1,
            grid=(width // tile,),
            in_specs=[
                pl.BlockSpec((rows, depth), lambda t, *_: (0, 0)),
                pl.BlockSpec((depth, tile), lambda t, meta: (meta[0], t)),
                pl.BlockSpec((rows, tile), lambda t, *_: (0, t)),
            ],
            out_specs=[pl.BlockSpec((per, tile), lambda t, *_: (0, t))] * parts,
        ),
        out_shape=[jax.ShapeDtypeStruct((per, width), bf16)] * parts,
        compiler_params=params(16),
        cost_estimate=cost(2 * rows * depth * width, depth * width * 2),
        name="down_unpack",
    )(meta, active, w_down, before)


def finish_kernel(lengths, where_side, mixed_ref, *refs):
    blocks, out_ref = refs[:-1], refs[-1]
    sides = len(blocks)
    slots, width = out_ref.shape
    step = width // sides
    live, rank = live_ranks(lengths, slots)
    row = lax.broadcasted_iota(i32, (PAD, PAD), 0)
    column = lax.broadcasted_iota(i32, (PAD, PAD), 1)
    pick = jnp.zeros((PAD, PAD), f32)
    for slot in range(slots):
        chosen = jnp.logical_and(column == rank[slot], row == slot)
        pick = jnp.where(jnp.logical_and(chosen, live[slot]), 1.0, pick)
    pick = pick.astype(bf16)
    for shift in range(sides):
        at = pl.multiple_of(lax.rem(where_side[0] + shift, sides) * step, step)
        back = jnp.dot(pick, blocks[shift][...], preferred_element_type=f32)[:slots]
        out_ref[:, pl.ds(at, step)] = (mixed_ref[:, pl.ds(at, step)] + back).astype(bf16)


def finish(ctx_len, side, mixed, blocks):
    whole = pl.BlockSpec(memory_space=pltpu.VMEM)
    scalars = pl.BlockSpec(memory_space=pltpu.SMEM)
    return pl.pallas_call(
        finish_kernel,
        in_specs=[scalars, scalars, whole] + [whole] * len(blocks),
        out_specs=whole,
        out_shape=jax.ShapeDtypeStruct(mixed.shape, bf16),
        compiler_params=params(16),
        cost_estimate=cost(mixed.size * 32, mixed.size * 8),
        name="finish",
    )(ctx_len, side, mixed, *blocks)


def swap(x, axis, count, mask):
    return lax.ppermute(x, axis, [(j, j ^ mask) for j in range(count)])


def shifted(x, axis, count, shift):
    return lax.ppermute(x, axis, [(j, (j + shift) % count) for j in range(count)])


def added(a, b):
    return (a.astype(f32) + b.astype(f32)).astype(bf16)


def tie(x, *others):
    return lax.optimization_barrier((x, *others))[0]


def feed_forward(rows, meta_of, gathered, w_up, w_down):
    width = w_up.shape[1] // 4
    packed, far_partner = pack_up(meta_of(3), gathered, w_up, rows, width)
    met = swap(far_partner, "side", 4, 1)
    near = up(meta_of(1), packed, w_up, width, bf16)
    far = up(meta_of(2), packed, w_up, width, bf16)
    own = up(meta_of(0), packed, w_up, width, f32)
    pair_sum = added(far, met)
    crossed = swap(pair_sum, "side", 4, 2)
    near = swap(tie(near, met), "side", 4, 1)
    lifted = own + near.astype(f32) + crossed.astype(f32)
    clipped = jnp.maximum(lifted, 0.0)
    active = (clipped * clipped).astype(bf16)
    across = swap(active, "side", 4, 2)
    beside = swap(active, "side", 4, 1)
    forwarded = swap(across, "side", 4, 1)
    total = down(meta_of(0), active, w_down, None)
    total = down(meta_of(1), beside, w_down, total)
    total = down(meta_of(2), across, w_down, total)
    return down_unpack(meta_of(3), forwarded, w_down, total, len(gathered), gathered[0].shape[0])


def line_shards(
    queries, new_kv, kv_pool, page_table, ctx_len, residual_in, norm_gain, w_up, w_down
):
    i, s = lax.axis_index("side"), lax.axis_index("shard")
    side = i.reshape(1)
    count = jnp.sum((ctx_len > 0).astype(i32))
    counts = lax.all_gather(count.reshape(1), ("side", "shard"), axis=0, tiled=True)
    mixed, *sends = attend(
        queries, new_kv, kv_pool, page_table, ctx_len, residual_in, norm_gain, side, 4
    )
    arrived = {shift: shifted(sends[shift], "side", 4, shift) for shift in (2, 1, 3)}
    arrived[0] = sends[0]
    here = jnp.concatenate([arrived[shift] for shift in range(4)], axis=0)
    by_x = swap(here, "shard", 4, 2)
    by_core = swap(here, "shard", 4, 1)
    by_both = swap(by_x, "shard", 4, 1)
    gathered = [here, by_core, by_x, by_both]

    starts = jnp.cumsum(counts) - counts
    order = jnp.stack([((i - shift) % 4) * 4 + (s ^ q) for q in range(4) for shift in range(4)])
    layout = jnp.concatenate([starts[order], counts[order]])

    def meta_of(mask):
        return jnp.concatenate([(i ^ mask).reshape(1), layout]).astype(i32)

    rows = 4 * 4 * LIVE_CAP
    mine, for_core, for_x, for_both = feed_forward(rows, meta_of, gathered, w_up, w_down)
    back = swap(jnp.concatenate([for_core, for_both], axis=0), "shard", 4, 1)
    half = back.shape[0] // 2
    to_x = added(for_x, back[half:])
    kept = added(mine, back[:half])
    home = added(kept, swap(to_x, "shard", 4, 2)).reshape(4, PAD, -1)
    blocks = [home[0]] + [shifted(home[shift], "side", 4, -shift) for shift in (1, 2, 3)]
    return finish(ctx_len, side, mixed, blocks)


def attend_slots(queries, new_kv, pool_pages, page_rows, lengths):
    slot_count = queries.shape[0]
    positions = page_rows.shape[1] * pool_pages.shape[1]
    fetched = pool_pages[page_rows].reshape(slot_count, positions, 2, KV_HEADS, HEAD)
    fresh_kv = new_kv.reshape(slot_count, 2, KV_HEADS, HEAD)
    query_heads = queries.reshape(slot_count, KV_HEADS, GROUP, HEAD)
    score_scale = 1.0 / math.sqrt(HEAD)
    scores = (
        jnp.einsum("sgqd,slgd->sgql", query_heads, fetched[:, :, 0], preferred_element_type=f32)
        * score_scale
    )
    own_score = (
        jnp.einsum("sgqd,sgd->sgq", query_heads, fresh_kv[:, 0], preferred_element_type=f32)
        * score_scale
    )
    visible = (jnp.arange(positions, dtype=i32)[None, :] < lengths[:, None])[:, None, None, :]
    scores = jnp.where(visible, scores, -1e30)
    highest = jnp.maximum(jnp.max(scores, axis=-1), own_score)
    weights = jnp.where(visible, jnp.exp(scores - highest[..., None]), 0.0)
    own_weight = jnp.exp(own_score - highest)
    denominator = jnp.sum(weights, axis=-1) + own_weight
    probabilities = (weights / denominator[..., None]).astype(bf16)
    own_prob = (own_weight / denominator).astype(bf16).astype(f32)
    attended = jnp.einsum(
        "sgql,slgd->sgqd", probabilities, fetched[:, :, 1], preferred_element_type=f32
    )
    attended = attended + own_prob[..., None] * fresh_kv[:, 1].astype(f32)[:, :, None, :]
    return attended.reshape(slot_count, -1)


def any_shards(queries, new_kv, kv_pool, page_table, ctx_len, residual_in, norm_gain, w_up, w_down):
    attended = attend_slots(queries, new_kv, kv_pool, page_table, ctx_len)
    mixed_rows = residual_in.astype(f32) + attended
    mean_square = jnp.mean(mixed_rows * mixed_rows, axis=-1, keepdims=True)
    normed = (mixed_rows * lax.rsqrt(mean_square + epsilon) * norm_gain.astype(f32)).astype(bf16)
    live_mask = ctx_len > 0
    spread = lax.all_to_all(normed, "side", split_axis=1, concat_axis=0, tiled=True)
    up_partial = jnp.dot(
        lax.all_gather(spread, "shard", axis=0, tiled=True), w_up, preferred_element_type=f32
    )
    lifted = lax.psum(up_partial, "side")
    clipped = jnp.maximum(lifted, 0.0)
    active = (clipped * clipped).astype(bf16)
    down_share = lax.psum_scatter(
        jnp.dot(active, w_down, preferred_element_type=f32).astype(bf16),
        "shard",
        scatter_dimension=0,
        tiled=True,
    )
    returned = lax.all_to_all(down_share, "side", split_axis=0, concat_axis=1, tiled=True)
    returned = jnp.where(live_mask[:, None], returned.astype(f32), 0.0)
    return (mixed_rows + returned).astype(bf16)


def solution(mesh):
    rows = ("grp", "side", "shard")
    placed = (
        P(rows, None),
        P(rows, None),
        P(rows, None, None),
        P(rows, None),
        P(rows),
        P(rows, None),
        P(),
        P("side", "shard"),
        P("shard", "side"),
    )
    square = mesh.shape["side"] == 4 and mesh.shape["shard"] == 4
    return jax.shard_map(
        line_shards if square else any_shards,
        mesh=mesh,
        in_specs=placed,
        out_specs=P(rows, None),
        check_vma=False,
    )
```

time: 270 us -> 140 us (0.52)
  waiting for transfers between devices: 154 us -> 49.3 us
  Pallas kernels: 0 us -> 34.4 us
  blocking collectives: 39.4 us -> 10.3 us
  matrix products: 24.8 us -> 0 us
  starting transfers between devices: 4.7 us -> 20.6 us
  between operations: 14.4 us -> 0.24 us
  local copies, waits for them, and re-layouts: 28.2 us -> 23.1 us
    psum x1 -> x0, waiting for transfers between devices: 145 us -> none  [shards(): lifted = lax.psum(up_partial, 'side')]
    ppermute x0 -> x17, waiting for transfers between devices: none -> 49.3 us  [the longest x11 40.5 us: swap(): return lax.ppermute(x, axis, [(j, j ^ mask) for j in range(count)])]
    pallas_call x0 -> x10, Pallas kernels: none -> 34.4 us  [the longest x1 9.12 us: attend(): pl.pallas_call(attend_kernel, grid_spec=pltpu.PrefetchScalarGridSpec(num_...]
    dot_general x5 -> x0, matrix products: 24.8 us -> none  [the longest x1 11.2 us: shards(): jnp.dot(active, w_down, preferred_element_type=jnp.float32)]
    ppermute x0 -> x17, starting transfers between devices: none -> 20.6 us  [the longest x6 10.5 us: shifted(): lax.ppermute(x, axis, [(j, (j + shift) % count) for j in range(count)])]
    all_to_all x1 -> x0, blocking collectives: 15.2 us -> none  [shards(): lax.all_to_all(normed, 'side', split_axis=1, concat_axis=0, tiled=True)]
    gather x1 -> x2, local copies, waits for them, and re-layouts: 12.4 us -> 1.32 us  [line_shards(): layout = jnp.concatenate([starts[order], counts[order]])]
    all_gather x1 -> x0, blocking collectives: 9.79 us -> none  [shards(): lax.all_gather(spread, 'shard', axis=0, tiled=True)]
  transfers between devices with their start and end apart: 3 -> 17, of which waited for: 2 -> 13; matrix products, arithmetic and copies ran while one was open for 0% -> 3% of each run, Pallas kernels for 0% -> 12%
where the time goes in v1:
time: 140 us; the launch traced here: 139 us
  waiting for transfers between devices  49.3 us (35%)
  Pallas kernels  34.4 us (25%)
  local copies, waits for them, and re-layouts  23.1 us (16%)
  starting transfers between devices  20.6 us (15%)
  blocking collectives  10.3 us (7%)
  other arithmetic  1.48 us (1%)
    ppermute x11, waiting for transfers between devices, swap(): return lax.ppermute(x, axis, [(j, j ^ mask) for j in range(count)])  40.5 us
    unnamed x34, local copies, waits for them, and re-layouts  20.8 us
    ppermute x6, starting transfers between devices, shifted(): lax.ppermute(x, axis, [(j, (j + shift) % count) for j in range(count)])  10.5 us
    unnamed x1, blocking collectives  10.3 us
    ppermute x11, starting transfers between devices, swap(): return lax.ppermute(x, axis, [(j, j ^ mask) for j in range(count)])  10.1 us
    pallas_call x1, Pallas kernels, attend(): pl.pallas_call(attend_kernel, grid_spec=pltpu.PrefetchScalarGridSpec(num_...  9.12 us
    ppermute x6, waiting for transfers between devices, shifted(): lax.ppermute(x, axis, [(j, (j + shift) % count) for j in range(count)])  8.81 us
    pallas_call x3, Pallas kernels, up(): pl.pallas_call(up_kernel, grid_spec=pltpu.PrefetchScalarGridSpec(num_scal...  8.53 us
  transfers between devices with their start and end apart: 17, of which 13 were waited for; matrix products, arithmetic and copies ran while one was open for 3% of the time, Pallas kernels for 12%

profile of v1, /device:TPU:0, one launch (start us, length us, event | category | flops | bytes accessed | tf_op | source)
XLA Modules:
  0.0 139.4 jit_solution(17664038737910011763)
XLA Ops:
  0.0 0.7 reshape.676.gain_ref
  0.8 3.1 %copy-done.2 = bf16[112,16,2048]{2,1,0:T(8,128)(2,1)S(1)} copy-done((bf16[112,16,2048]{2,1,0:T(8,128)(2,1)S(1)}, bf16[112,16,2048]{2,1,0:T(8,128)(2,1)}, u32[]{:S(2)}) %copy-start.2) | copy-done | bytes 7340056
  3.8 0.9 copy-done.3
  4.8 0.9 copy-done.4
  5.7 0.8 copy-done.5
  6.6 0.7 copy-done.6
  7.3 0.7 copy-done.7
  7.9 9.1 %attend.1 = (f32[15,8192]{1,0:T(8,128)S(1)}, bf16[16,2048]{1,0:T(8,128)(2,1)S(1)}, bf16[16,2048]{1,0:T(8,128)(2,1)S(1)}, bf16[16,2048]{1,0:T(8,128)(2,1)S(1)}, bf16[16,2048]{1,0:T(8,128)(2,1)S(1)}) custom-call(s32[15]{0:T(128)S(1)} %copy-done.7, s32[1]{0:T(128)} %bitcast.where_side, bf16[15,8192]{1,0:T(8,128)(2,1)S(1)} %copy-done.3, ...), custom_call_target="tpu_custom_call" | custom-call | flops 939524096 | bytes 7340032 | tf_op jit(solution)/shard_map/attend/pallas_call | solution.py:138
  17.1 3.1 %collective-permute-start = (bf16[16,2048]{1,0:T(8,128)(2,1)S(1)}, bf16[16,2048]{1,0:T(8,128)(2,1)S(1)}, u32[]{:S(2)}, u32[]{:S(2)}) collective-permute-start(bf16[16,2048]{1,0:T(8,128)(2,1)S(1)} %get-tuple-element.19), channel_id=1, source_target_pairs={{0,4},{4,8},{8,12},{12,0},{1,5},{5,9},{9,13},{13,1},{2,6},{6,10},{... | collective-permute-start | bytes 196616 | tf_op jit(solution)/shard_map/ppermute | solution.py:358
  20.1 2.6 %collective-permute-start.1 = (bf16[16,2048]{1,0:T(8,128)(2,1)S(1)}, bf16[16,2048]{1,0:T(8,128)(2,1)S(1)}, u32[]{:S(2)}, u32[]{:S(2)}) collective-permute-start(bf16[16,2048]{1,0:T(8,128)(2,1)S(1)} %get-tuple-element.20), channel_id=1, source_target_pairs={{0,8},{4,12},{8,0},{12,4},{1,9},{5,13},{9,1},{13,5},{2,10},{6,14},... | collective-permute-start | bytes 196616 | tf_op jit(solution)/shard_map/ppermute | solution.py:358
  22.7 1.3 collective-permute-start.2
  24.1 0.6 collective-permute-done
  24.7 2.5 %collective-permute-done.1 = bf16[16,2048]{1,0:T(8,128)(2,1)S(1)} collective-permute-done((bf16[16,2048]{1,0:T(8,128)(2,1)S(1)}, bf16[16,2048]{1,0:T(8,128)(2,1)S(1)}, u32[]{:S(2)}, u32[]{:S(2)}) %collective-permute-start.1) | collective-permute-done | bytes 65568 | tf_op jit(solution)/shard_map/ppermute | solution.py:358
  27.4 1.6 %collective-permute-start.4 = (bf16[64,2048]{1,0:T(8,128)(2,1)S(1)}, bf16[64,2048]{1,0:T(8,128)(2,1)S(1)}, u32[]{:S(2)}, u32[]{:S(2)}) collective-permute-start(bf16[64,2048]{1,0:T(8,128)(2,1)S(1)} %constant_dynamic-update-slice_fusion.refs_0_), channel_id=1, source_target_pairs={{0,2},{1,3},{2,0},{3,1},{4,6},{5,7},{6,4},{7,5},{8,10},{9,11},{10,... | collective-permute-start | bytes 786440 | tf_op jit(solution)/shard_map/ppermute | solution.py:354
  29.1 0.6 dynamic-slice
  29.7 0.6 fusion
  30.3 1.4 %dynamic-update-slice = s32[16]{0:T(128)S(1)} dynamic-update-slice(s32[16]{0:T(128)S(1)} %broadcast.30, s32[1]{0:T(128)} %bitcast.2, u32[]{:T(128)} %bitcast.3) | dynamic-update-slice | bytes 12
  32.0 3.4 %collective-permute-done.4.refs_2_ = bf16[64,2048]{1,0:T(8,128)(2,1)S(1)} collective-permute-done((bf16[64,2048]{1,0:T(8,128)(2,1)S(1)}, bf16[64,2048]{1,0:T(8,128)(2,1)S(1)}, u32[]{:S(2)}, u32[]{:S(2)}) %collective-permute-start.4) | collective-permute-done | bytes 262176 | tf_op jit(solution)/shard_map/ppermute | solution.py:354
  35.3 10.3 %all-reduce = s32[16]{0:T(128)S(1)} all-reduce(s32[16]{0:T(128)S(1)} %dynamic-update-slice), channel_id=1, replica_groups=mesh['grp'=2,'side'=4,'shard'=4] {'side','shard'}, use_global_device_ids=true, to_apply=%add | all-reduce | flops 16 | bytes 128
  45.9 0.7 gather_fusion.1
  46.5 0.7 gather_fusion
  47.3 5.8 %copy-done = bf16[2048,4096]{1,0:T(8,128)(2,1)S(1)} copy-done((bf16[2048,4096]{1,0:T(8,128)(2,1)S(1)}, bf16[2048,4096]{1,0:T(8,128)(2,1)}, u32[]{:S(2)}) %copy-start) | copy-done | bytes 16777240
  53.1 3.7 %pack_up.1 = (bf16[192,2048]{1,0:T(8,128)(2,1)S(1)}, bf16[192,1024]{1,0:T(8,128)(2,1)S(1)}) custom-call(s32[33]{0:T(128)S(1)} %add_add_fusion.meta, bf16[64,2048]{1,0:T(8,128)(2,1)S(1)} %constant_dynamic-update-slice_fusion.refs_0_, bf16[64,2048]{1,0:T(8,128)(2,1)S(1)} %collective-permute-done.3.refs_1_, ...), custom_call_target="tpu_custom_call" | custom-call | flops 805306368 | bytes 4194304 | tf_op jit(solution)/shard_map/pack_up/pallas_call | solution.py:205
  56.8 0.5 collective-permute-start.6
  57.4 5.8 %copy-done.1 = bf16[2048,4096]{1,0:T(8,128)(2,1)S(1)} copy-done((bf16[2048,4096]{1,0:T(8,128)(2,1)S(1)}, bf16[2048,4096]{1,0:T(8,128)(2,1)}, u32[]{:S(2)}) %copy-start.1) | copy-done | bytes 16777240
  63.2 2.8 %up.4 = bf16[192,1024]{1,0:T(8,128)(2,1)S(1)} custom-call(s32[33]{0:T(128)S(1)} %get-tuple-element.33.meta, bf16[192,2048]{1,0:T(8,128)(2,1)S(1)} %get-tuple-element.22.x_ref, bf16[2048,4096]{1,0:T(8,128)(2,1)S(1)} %copy-done.1), custom_call_target="tpu_custom_call" | custom-call | flops 805306368 | bytes 4194304 | tf_op jit(solution)/shard_map/up/pallas_call | solution.py:230
  66.0 2.9 %up.5 = bf16[192,1024]{1,0:T(8,128)(2,1)S(1)} custom-call(s32[33]{0:T(128)S(1)} %get-tuple-element.35.meta, bf16[192,2048]{1,0:T(8,128)(2,1)S(1)} %get-tuple-element.22.x_ref, bf16[2048,4096]{1,0:T(8,128)(2,1)S(1)} %copy-done.1), custom_call_target="tpu_custom_call" | custom-call | flops 805306368 | bytes 4194304 | tf_op jit(solution)/shard_map/up/pallas_call | solution.py:230
  68.9 1.6 %collective-permute-start.7 = (bf16[192,1024]{1,0:T(8,128)(2,1)S(1)}, bf16[192,1024]{1,0:T(8,128)(2,1)S(1)}, u32[]{:S(2)}, u32[]{:S(2)}) collective-permute-start(bf16[192,1024]{1,0:T(8,128)(2,1)S(1)} %up.4), channel_id=1, source_target_pairs={{0,4},{4,0},{8,12},{12,8},{1,5},{5,1},{9,13},{13,9},{2,6},{6,2},{1... | collective-permute-start | bytes 1179656 | tf_op jit(solution)/shard_map/ppermute | solution.py:354
  70.7 2.4 %collective-permute-start.8 = (bf16[192,1024]{1,0:T(8,128)(2,1)S(1)}, bf16[192,1024]{1,0:T(8,128)(2,1)S(1)}, u32[]{:S(2)}, u32[]{:S(2)}) collective-permute-start(bf16[192,1024]{1,0:T(8,128)(2,1)S(1)} %add_convert_fusion), channel_id=1, source_target_pairs={{0,8},{4,12},{8,0},{12,4},{1,9},{5,13},{9,1},{13,5},{2,10},{6,14},... | collective-permute-start | bytes 1179656 | tf_op jit(solution)/shard_map/ppermute | solution.py:354
  73.1 2.8 %up.3 = f32[192,1024]{1,0:T(8,128)S(1)} custom-call(s32[33]{0:T(128)S(1)} %get-tuple-element.34.meta, bf16[192,2048]{1,0:T(8,128)(2,1)S(1)} %get-tuple-element.22.x_ref, bf16[2048,4096]{1,0:T(8,128)(2,1)S(1)} %copy-done.1), custom_call_target="tpu_custom_call" | custom-call | flops 805306368 | bytes 4194304 | tf_op jit(solution)/shard_map/up/pallas_call | solution.py:230
  76.0 9.4 %collective-permute-done.7 = bf16[192,1024]{1,0:T(8,128)(2,1)S(1)} collective-permute-done((bf16[192,1024]{1,0:T(8,128)(2,1)S(1)}, bf16[192,1024]{1,0:T(8,128)(2,1)S(1)}, u32[]{:S(2)}, u32[]{:S(2)}) %collective-permute-start.7) | collective-permute-done | bytes 393248 | tf_op jit(solution)/shard_map/ppermute | solution.py:354
  85.3 8.0 %collective-permute-done.8 = bf16[192,1024]{1,0:T(8,128)(2,1)S(1)} collective-permute-done((bf16[192,1024]{1,0:T(8,128)(2,1)S(1)}, bf16[192,1024]{1,0:T(8,128)(2,1)S(1)}, u32[]{:S(2)}, u32[]{:S(2)}) %collective-permute-start.8) | collective-permute-done | bytes 393248 | tf_op jit(solution)/shard_map/ppermute | solution.py:354
  93.6 2.8 %collective-permute-start.11 = (bf16[192,1024]{1,0:T(8,128)(2,1)S(1)}, bf16[192,1024]{1,0:T(8,128)(2,1)S(1)}, u32[]{:S(2)}, u32[]{:S(2)}) collective-permute-start(bf16[192,1024]{1,0:T(8,128)(2,1)S(1)} %multiply_convert_fusion.refs_0_), channel_id=1, source_target_pairs={{0,4},{4,0},{8,12},{12,8},{1,5},{5,1},{9,13},{13,9},{2,6},{6,2},{1... | collective-permute-start | bytes 1179656 | tf_op jit(solution)/shard_map/ppermute | solution.py:354
  96.3 9.5 %collective-permute-done.9.refs_0_ = bf16[192,1024]{1,0:T(8,128)(2,1)S(1)} collective-permute-done((bf16[192,1024]{1,0:T(8,128)(2,1)S(1)}, bf16[192,1024]{1,0:T(8,128)(2,1)S(1)}, u32[]{:S(2)}, u32[]{:S(2)}) %collective-permute-start.9) | collective-permute-done | bytes 393248 | tf_op jit(solution)/shard_map/ppermute | solution.py:354
  105.9 2.5 %down.3.refs_2_ = f32[192,2048]{1,0:T(8,128)S(1)} custom-call(s32[33]{0:T(128)S(1)} %get-tuple-element.34.meta, bf16[192,1024]{1,0:T(8,128)(2,1)S(1)} %multiply_convert_fusion.refs_0_, bf16[4096,2048]{1,0:T(8,128)(2,1)S(1)} %bitcast.26), custom_call_target="tpu_custom_call" | custom-call | flops 805306368 | bytes 4194304 | tf_op jit(solution)/shard_map/down/pallas_call | solution.py:260
  108.5 0.7 collective-permute-done.11.refs_0_
  109.1 2.7 %down.4.refs_2_ = f32[192,2048]{1,0:T(8,128)S(1)} custom-call(s32[33]{0:T(128)S(1)} %get-tuple-element.33.meta, bf16[192,1024]{1,0:T(8,128)(2,1)S(1)} %collective-permute-done.11.refs_0_, bf16[4096,2048]{1,0:T(8,128)(2,1)S(1)} %bitcast.26, f32[192,2048]{1,0:T(8,128)S(1)} %down.3.refs_2_), custom_call_target="tpu_custom_call" | custom-call | flops 805306368 | bytes 4194304 | tf_op jit(solution)/shard_map/down/pallas_call | solution.py:260
  111.8 2.7 %down.5.before_ref = f32[192,2048]{1,0:T(8,128)S(1)} custom-call(s32[33]{0:T(128)S(1)} %get-tuple-element.35.meta, bf16[192,1024]{1,0:T(8,128)(2,1)S(1)} %collective-permute-done.9.refs_0_, bf16[4096,2048]{1,0:T(8,128)(2,1)S(1)} %bitcast.26, f32[192,2048]{1,0:T(8,128)S(1)} %down.4.refs_2_), custom_call_target="tpu_custom_call" | custom-call | flops 805306368 | bytes 4194304 | tf_op jit(solution)/shard_map/down/pallas_call | solution.py:260
  114.7 3.6 %down_unpack.1 = (bf16[64,2048]{1,0:T(8,128)(2,1)S(1)}, bf16[64,2048]{1,0:T(8,128)(2,1)S(1)}, bf16[64,2048]{1,0:T(8,128)(2,1)S(1)}, bf16[64,2048]{1,0:T(8,128)(2,1)S(1)}) custom-call(s32[33]{0:T(128)S(1)} %add_add_fusion.meta, bf16[192,1024]{1,0:T(8,128)(2,1)S(1)} %collective-permute-done.10.a_ref, bf16[4096,2048]{1,0:T(8,128)(2,1)S(1)} %bitcast.26, ...), custom_call_target="tpu_custom_call" | custom-call | flops 805306368 | bytes 4194304 | tf_op jit(solution)/shard_map/down_unpack/pallas_call | solution.py:301
  118.5 1.9 %collective-permute-done.12 = bf16[128,2048]{1,0:T(8,128)(2,1)S(1)} collective-permute-done((bf16[128,2048]{1,0:T(8,128)(2,1)S(1)}, bf16[128,2048]{1,0:T(8,128)(2,1)S(1)}, u32[]{:S(2)}, u32[]{:S(2)}) %collective-permute-start.12) | collective-permute-done | bytes 524320 | tf_op jit(solution)/shard_map/ppermute | solution.py:354
  120.4 1.0 collective-permute-start.13
  121.4 7.4 %collective-permute-done.13 = bf16[64,2048]{1,0:T(8,128)(2,1)S(1)} collective-permute-done((bf16[64,2048]{1,0:T(8,128)(2,1)S(1)}, bf16[64,2048]{1,0:T(8,128)(2,1)S(1)}, u32[]{:S(2)}, u32[]{:S(2)}) %collective-permute-start.13) | collective-permute-done | bytes 262176 | tf_op jit(solution)/shard_map/ppermute | solution.py:354
  129.0 1.7 %collective-permute-start.14 = (bf16[16,2048]{1,0:T(8,128)(2,1)S(1)}, bf16[16,2048]{1,0:T(8,128)(2,1)S(1)}, u32[]{:S(2)}, u32[]{:S(2)}) collective-permute-start(bf16[16,2048]{1,0:T(8,128)(2,1)S(1)} %get-tuple-element.31), channel_id=1, source_target_pairs={{0,12},{4,0},{8,4},{12,8},{1,13},{5,1},{9,5},{13,9},{2,14},{6,2},{... | collective-permute-start | bytes 196616 | tf_op jit(solution)/shard_map/ppermute | solution.py:358
  130.7 1.0 collective-permute-start.15
  131.7 0.8 collective-permute-start.16
  132.5 0.8 collective-permute-done.14.refs_1_
  133.3 4.6 %collective-permute-done.15.refs_2_ = bf16[16,2048]{1,0:T(8,128)(2,1)S(1)} collective-permute-done((bf16[16,2048]{1,0:T(8,128)(2,1)S(1)}, bf16[16,2048]{1,0:T(8,128)(2,1)S(1)}, u32[]{:S(2)}, u32[]{:S(2)}) %collective-permute-start.15) | collective-permute-done | bytes 65568 | tf_op jit(solution)/shard_map/ppermute | solution.py:358
  137.9 1.5 %finish.1 = bf16[15,8192]{1,0:T(8,128)(2,1)} custom-call(s32[15]{0:T(128)S(1)} %copy-done.8, s32[1]{0:T(128)} %bitcast.where_side, f32[15,8192]{1,0:T(8,128)S(1)} %get-tuple-element.17.mixed_ref, bf16[16,2048]{1,0:T(8,128)(2,1)S(1)} %get-tuple-element.32.refs_0_, bf16[16,2048]{1,0:T(8,128)(2,1)S(1)} %collective-permute-done.14.refs_1_, ...), custom_call_target="tpu_custom_call" | custom-call | flops 3932160 | bytes 983040 | tf_op jit(solution)/shard_map/finish/pallas_call | solution.py:342
  (52 shorter events, 1.8 us)
Async XLA Ops:
  0.7 3.1 %copy-start.2 = (bf16[112,16,2048]{2,1,0:T(8,128)(2,1)S(1)}, bf16[112,16,2048]{2,1,0:T(8,128)(2,1)}, u32[]{:S(2)}) copy-start(bf16[112,16,2048]{2,1,0:T(8,128)(2,1)} %v_ref.1) | copy-start | bytes 22020100
  3.8 0.9 copy-start.3
  4.8 0.9 copy-start.4
  5.7 0.8 copy-start.5
  6.6 0.7 copy-start.6
  7.3 0.7 copy-start.7
  7.9 21.1 %copy-start.9 = (u32[32]{0:T(128)S(1)}, u32[32]{0:T(128)}, u32[]{:S(2)}) copy-start(u32[32]{0:T(128)} %constant.85) | copy-start | bytes 388
  7.9 21.8 %copy-start.8 = (s32[15]{0:T(128)S(1)}, s32[15]{0:T(128)}, u32[]{:S(2)}) copy-start(s32[15]{0:T(128)} %lengths.3) | copy-start | bytes 184
  17.1 7.6 %collective-permute-start = (bf16[16,2048]{1,0:T(8,128)(2,1)S(1)}, bf16[16,2048]{1,0:T(8,128)(2,1)S(1)}, u32[]{:S(2)}, u32[]{:S(2)}) collective-permute-start(bf16[16,2048]{1,0:T(8,128)(2,1)S(1)} %get-tuple-element.19), channel_id=1, source_target_pairs={{0,4},{4,8},{8,12},{12,0},{1,5},{5,9},{9,13},{13,1},{2,6},{6,10},{... | collective-permute-start | bytes 196616 | tf_op jit(solution)/shard_map/ppermute | solution.py:358
  20.1 7.1 %collective-permute-start.1 = (bf16[16,2048]{1,0:T(8,128)(2,1)S(1)}, bf16[16,2048]{1,0:T(8,128)(2,1)S(1)}, u32[]{:S(2)}, u32[]{:S(2)}) collective-permute-start(bf16[16,2048]{1,0:T(8,128)(2,1)S(1)} %get-tuple-element.20), channel_id=1, source_target_pairs={{0,8},{4,12},{8,0},{12,4},{1,9},{5,13},{9,1},{13,5},{2,10},{6,14},... | collective-permute-start | bytes 196616 | tf_op jit(solution)/shard_map/ppermute | solution.py:358
  22.7 4.7 %collective-permute-start.2 = (bf16[16,2048]{1,0:T(8,128)(2,1)S(1)}, bf16[16,2048]{1,0:T(8,128)(2,1)S(1)}, u32[]{:S(2)}, u32[]{:S(2)}) collective-permute-start(bf16[16,2048]{1,0:T(8,128)(2,1)S(1)} %get-tuple-element.21), channel_id=1, source_target_pairs={{0,12},{4,0},{8,4},{12,8},{1,13},{5,1},{9,5},{13,9},{2,14},{6,2},{... | collective-permute-start | bytes 196616 | tf_op jit(solution)/shard_map/ppermute | solution.py:358
  27.4 7.9 %collective-permute-start.4 = (bf16[64,2048]{1,0:T(8,128)(2,1)S(1)}, bf16[64,2048]{1,0:T(8,128)(2,1)S(1)}, u32[]{:S(2)}, u32[]{:S(2)}) collective-permute-start(bf16[64,2048]{1,0:T(8,128)(2,1)S(1)} %constant_dynamic-update-slice_fusion.refs_0_), channel_id=1, source_target_pairs={{0,2},{1,3},{2,0},{3,1},{4,6},{5,7},{6,4},{7,5},{8,10},{9,11},{10,... | collective-permute-start | bytes 786440 | tf_op jit(solution)/shard_map/ppermute | solution.py:354
  31.9 15.4 %collective-permute-start.3 = (bf16[64,2048]{1,0:T(8,128)(2,1)S(1)}, bf16[64,2048]{1,0:T(8,128)(2,1)S(1)}, u32[]{:S(2)}, u32[]{:S(2)}) collective-permute-start(bf16[64,2048]{1,0:T(8,128)(2,1)S(1)} %constant_dynamic-update-slice_fusion.refs_0_), channel_id=1, source_target_pairs={{0,1},{1,0},{2,3},{3,2},{4,5},{5,4},{6,7},{7,6},{8,9},{9,8},{10,11... | collective-permute-start | bytes 786440 | tf_op jit(solution)/shard_map/ppermute | solution.py:354
  35.3 12.0 %collective-permute-start.5 = (bf16[64,2048]{1,0:T(8,128)(2,1)S(1)}, bf16[64,2048]{1,0:T(8,128)(2,1)S(1)}, u32[]{:S(2)}, u32[]{:S(2)}) collective-permute-start(bf16[64,2048]{1,0:T(8,128)(2,1)S(1)} %collective-permute-done.4.refs_2_), channel_id=1, source_target_pairs={{0,1},{1,0},{2,3},{3,2},{4,5},{5,4},{6,7},{7,6},{8,9},{9,8},{10,11... | collective-permute-start | bytes 786440 | tf_op jit(solution)/shard_map/ppermute | solution.py:354
  47.3 5.8 %copy-start = (bf16[2048,4096]{1,0:T(8,128)(2,1)S(1)}, bf16[2048,4096]{1,0:T(8,128)(2,1)}, u32[]{:S(2)}) copy-start(bf16[2048,4096]{1,0:T(8,128)(2,1)} %w_ref.6) | copy-start | bytes 50331652
  56.8 12.1 %collective-permute-start.6 = (bf16[192,1024]{1,0:T(8,128)(2,1)S(1)}, bf16[192,1024]{1,0:T(8,128)(2,1)S(1)}, u32[]{:S(2)}, u32[]{:S(2)}) collective-permute-start(bf16[192,1024]{1,0:T(8,128)(2,1)S(1)} %get-tuple-element.23), channel_id=1, source_target_pairs={{0,4},{4,0},{8,12},{12,8},{1,5},{5,1},{9,13},{13,9},{2,6},{6,2},{1... | collective-permute-start | bytes 1179656 | tf_op jit(solution)/shard_map/ppermute | solution.py:354
  57.4 5.8 %copy-start.1 = (bf16[2048,4096]{1,0:T(8,128)(2,1)S(1)}, bf16[2048,4096]{1,0:T(8,128)(2,1)}, u32[]{:S(2)}) copy-start(bf16[2048,4096]{1,0:T(8,128)(2,1)} %w_ref.6) | copy-start | bytes 50331652
  66.0 39.8 %slice-start = ((s8[16777216]{0:T(1024)(128)(4,1)}), s8[4194304]{0:T(1024)(128)(4,1)S(1)}, s32[]{:S(2)}) async-start(s8[16777216]{0:T(1024)(128)(4,1)} %bitcast.25), calls=%async_computation | async-start | bytes 8388608
  66.0 39.8 %slice-start.1 = ((s8[16777216]{0:T(1024)(128)(4,1)}), s8[4194304]{0:T(1024)(128)(4,1)S(1)}, s32[]{:S(2)}) async-start(s8[16777216]{0:T(1024)(128)(4,1)} %bitcast.25), calls=%async_computation.1 | async-start | bytes 8388608
  68.9 16.4 %collective-permute-start.7 = (bf16[192,1024]{1,0:T(8,128)(2,1)S(1)}, bf16[192,1024]{1,0:T(8,128)(2,1)S(1)}, u32[]{:S(2)}, u32[]{:S(2)}) collective-permute-start(bf16[192,1024]{1,0:T(8,128)(2,1)S(1)} %up.4), channel_id=1, source_target_pairs={{0,4},{4,0},{8,12},{12,8},{1,5},{5,1},{9,13},{13,9},{2,6},{6,2},{1... | collective-permute-start | bytes 1179656 | tf_op jit(solution)/shard_map/ppermute | solution.py:354
  70.7 22.6 %collective-permute-start.8 = (bf16[192,1024]{1,0:T(8,128)(2,1)S(1)}, bf16[192,1024]{1,0:T(8,128)(2,1)S(1)}, u32[]{:S(2)}, u32[]{:S(2)}) collective-permute-start(bf16[192,1024]{1,0:T(8,128)(2,1)S(1)} %add_convert_fusion), channel_id=1, source_target_pairs={{0,8},{4,12},{8,0},{12,4},{1,9},{5,13},{9,1},{13,5},{2,10},{6,14},... | collective-permute-start | bytes 1179656 | tf_op jit(solution)/shard_map/ppermute | solution.py:354
  73.1 32.8 %slice-start.2 = ((s8[16777216]{0:T(1024)(128)(4,1)}), s8[4194304]{0:T(1024)(128)(4,1)S(1)}, s32[]{:S(2)}) async-start(s8[16777216]{0:T(1024)(128)(4,1)} %bitcast.25), calls=%async_computation.2 | async-start | bytes 8388608
  73.1 32.8 %slice-start.3 = ((s8[16777216]{0:T(1024)(128)(4,1)}), s8[4194304]{0:T(1024)(128)(4,1)S(1)}, s32[]{:S(2)}) async-start(s8[16777216]{0:T(1024)(128)(4,1)} %bitcast.25), calls=%async_computation.3 | async-start | bytes 8388608
  93.5 12.4 %collective-permute-start.9 = (bf16[192,1024]{1,0:T(8,128)(2,1)S(1)}, bf16[192,1024]{1,0:T(8,128)(2,1)S(1)}, u32[]{:S(2)}, u32[]{:S(2)}) collective-permute-start(bf16[192,1024]{1,0:T(8,128)(2,1)S(1)} %multiply_convert_fusion.refs_0_), channel_id=1, source_target_pairs={{0,8},{4,12},{8,0},{12,4},{1,9},{5,13},{9,1},{13,5},{2,10},{6,14},... | collective-permute-start | bytes 1179656 | tf_op jit(solution)/shard_map/ppermute | solution.py:354
  93.6 15.6 %collective-permute-start.11 = (bf16[192,1024]{1,0:T(8,128)(2,1)S(1)}, bf16[192,1024]{1,0:T(8,128)(2,1)S(1)}, u32[]{:S(2)}, u32[]{:S(2)}) collective-permute-start(bf16[192,1024]{1,0:T(8,128)(2,1)S(1)} %multiply_convert_fusion.refs_0_), channel_id=1, source_target_pairs={{0,4},{4,0},{8,12},{12,8},{1,5},{5,1},{9,13},{13,9},{2,6},{6,2},{1... | collective-permute-start | bytes 1179656 | tf_op jit(solution)/shard_map/ppermute | solution.py:354
  105.9 8.9 %collective-permute-start.10 = (bf16[192,1024]{1,0:T(8,128)(2,1)S(1)}, bf16[192,1024]{1,0:T(8,128)(2,1)S(1)}, u32[]{:S(2)}, u32[]{:S(2)}) collective-permute-start(bf16[192,1024]{1,0:T(8,128)(2,1)S(1)} %collective-permute-done.9.refs_0_), channel_id=1, source_target_pairs={{0,4},{4,0},{8,12},{12,8},{1,5},{5,1},{9,13},{13,9},{2,6},{6,2},{1... | collective-permute-start | bytes 1179656 | tf_op jit(solution)/shard_map/ppermute | solution.py:354
  118.4 2.0 %collective-permute-start.12 = (bf16[128,2048]{1,0:T(8,128)(2,1)S(1)}, bf16[128,2048]{1,0:T(8,128)(2,1)S(1)}, u32[]{:S(2)}, u32[]{:S(2)}) collective-permute-start(bf16[128,2048]{1,0:T(8,128)(2,1)S(1)} %pad_maximum_fusion), channel_id=1, source_target_pairs={{0,1},{1,0},{2,3},{3,2},{4,5},{5,4},{6,7},{7,6},{8,9},{9,8},{10,11... | collective-permute-start | bytes 1572872 | tf_op jit(solution)/shard_map/ppermute | solution.py:354
  120.4 8.4 %collective-permute-start.13 = (bf16[64,2048]{1,0:T(8,128)(2,1)S(1)}, bf16[64,2048]{1,0:T(8,128)(2,1)S(1)}, u32[]{:S(2)}, u32[]{:S(2)}) collective-permute-start(bf16[64,2048]{1,0:T(8,128)(2,1)S(1)} %add_convert_fusion.2), channel_id=1, source_target_pairs={{0,2},{1,3},{2,0},{3,1},{4,6},{5,7},{6,4},{7,5},{8,10},{9,11},{10,... | collective-permute-start | bytes 786440 | tf_op jit(solution)/shard_map/ppermute | solution.py:354
  129.0 4.3 %collective-permute-start.14 = (bf16[16,2048]{1,0:T(8,128)(2,1)S(1)}, bf16[16,2048]{1,0:T(8,128)(2,1)S(1)}, u32[]{:S(2)}, u32[]{:S(2)}) collective-permute-start(bf16[16,2048]{1,0:T(8,128)(2,1)S(1)} %get-tuple-element.31), channel_id=1, source_target_pairs={{0,12},{4,0},{8,4},{12,8},{1,13},{5,1},{9,5},{13,9},{2,14},{6,2},{... | collective-permute-start | bytes 196616 | tf_op jit(solution)/shard_map/ppermute | solution.py:358
  130.7 7.2 %collective-permute-start.15 = (bf16[16,2048]{1,0:T(8,128)(2,1)S(1)}, bf16[16,2048]{1,0:T(8,128)(2,1)S(1)}, u32[]{:S(2)}, u32[]{:S(2)}) collective-permute-start(bf16[16,2048]{1,0:T(8,128)(2,1)S(1)} %get-tuple-element.30), channel_id=1, source_target_pairs={{0,8},{4,12},{8,0},{12,4},{1,9},{5,13},{9,1},{13,5},{2,10},{6,14},... | collective-permute-start | bytes 196616 | tf_op jit(solution)/shard_map/ppermute | solution.py:358
  131.7 6.3 %collective-permute-start.16 = (bf16[16,2048]{1,0:T(8,128)(2,1)S(1)}, bf16[16,2048]{1,0:T(8,128)(2,1)S(1)}, u32[]{:S(2)}, u32[]{:S(2)}) collective-permute-start(bf16[16,2048]{1,0:T(8,128)(2,1)S(1)} %get-tuple-element.29), channel_id=1, source_target_pairs={{0,4},{4,8},{8,12},{12,0},{1,5},{5,9},{9,13},{13,1},{2,6},{6,10},{... | collective-permute-start | bytes 196616 | tf_op jit(solution)/shard_map/ppermute | solution.py:358

commit v2 on v1

--- a/solution.py
+++ b/solution.py
@@ -112,6 +112,7 @@
     @pl.when(head == KV_HEADS - 1)
     def _():
         live, rank = live_ranks(lengths, slots)
+        count = (rank[-1] + live[-1].astype(i32)).astype(f32)
         row = lax.broadcasted_iota(i32, (PAD, PAD), 0)
         column = lax.broadcasted_iota(i32, (PAD, PAD), 1)
         pick = jnp.zeros((PAD, PAD), f32)
@@ -125,7 +126,9 @@
             at = pl.multiple_of(lax.rem(where_side[0] + shift, sides) * step, step)
             normed = mixed_ref[:, pl.ds(at, step)] * root * gain_ref[:, pl.ds(at, step)].astype(f32)
             normed = pad_rows(normed.astype(bf16))
-            sends[shift][...] = jnp.dot(pick, normed, preferred_element_type=f32).astype(bf16)
+            rows = jnp.dot(pick, normed, preferred_element_type=f32)
+            last = lax.broadcasted_iota(i32, rows.shape, 0) == PAD - 1
+            sends[shift][...] = jnp.where(last, count, rows).astype(bf16)
 
 
 def attend(queries, new_kv, kv_pool, page_table, ctx_len, residual_in, norm_gain, side, sides):
@@ -165,7 +168,7 @@
     )
 
 
-def pack_up_kernel(meta, *refs, parts):
+def pack_up_kernel(side, layout, *refs, parts):
     gathered, w_ref, packed_ref, out_ref = refs[:parts], refs[parts], refs[-2], refs[-1]
     rows = packed_ref.shape[0]
 
@@ -179,8 +182,8 @@
             row = lax.broadcasted_iota(i32, (rows, per), 0)
             target = jnp.full((rows, per), -1, i32)
             for piece in range(pieces):
-                base = meta[1 + part * pieces + piece]
-                count = meta[1 + parts * pieces + part * pieces + piece]
+                base = layout[part * pieces + piece]
+                count = layout[(parts + part) * pieces + piece]
                 inside = lane - piece * PAD
                 mine = jnp.logical_and(inside >= 0, inside < count)
                 target = jnp.where(mine, base + inside, target)
@@ -191,24 +194,24 @@
     out_ref[...] = jnp.dot(packed_ref[...], w_ref[...], preferred_element_type=f32).astype(out_ref.dtype)
 
 
-def up_kernel(meta, x_ref, w_ref, out_ref):
+def up_kernel(side, x_ref, w_ref, out_ref):
     out_ref[...] = jnp.dot(x_ref[...], w_ref[...], preferred_element_type=f32).astype(out_ref.dtype)
 
 
 TILE = 256
 
 
-def pack_up(meta, gathered, w_up, rows, block_width):
+def pack_up(side, layout, gathered, w_up, rows, block_width, mask):
     depth = w_up.shape[0]
     tiles = block_width // TILE
     fixed = lambda t, *_: (0, 0)
     return pl.pallas_call(
         functools.partial(pack_up_kernel, parts=len(gathered)),
         grid_spec=pltpu.PrefetchScalarGridSpec(
-            num_scalar_prefetch=1,
+            num_scalar_prefetch=2,
             grid=(tiles,),
             in_specs=[pl.BlockSpec(g.shape, fixed) for g in gathered]
-            + [pl.BlockSpec((depth, TILE), lambda t, meta: (0, meta[0] * tiles + t))],
+            + [pl.BlockSpec((depth, TILE), lambda t, side, *_: (0, (side[0] ^ mask) * tiles + t))],
             out_specs=[
                 pl.BlockSpec((rows, depth), fixed),
                 pl.BlockSpec((rows, TILE), lambda t, *_: (0, t)),
@@ -221,10 +224,10 @@
         compiler_params=params(24),
         cost_estimate=cost(2 * rows * depth * block_width, depth * block_width * 2),
         name="pack_up",
-    )(meta, *gathered, w_up)
-
-
-def up(meta, packed, w_up, block_width, dtype):
+    )(side, layout, *gathered, w_up)
+
+
+def up(side, packed, w_up, block_width, dtype, mask):
     rows, depth = packed.shape
     tiles = block_width // TILE
     return pl.pallas_call(
@@ -234,7 +237,7 @@
             grid=(tiles,),
             in_specs=[
                 pl.BlockSpec((rows, depth), lambda t, *_: (0, 0)),
-                pl.BlockSpec((depth, TILE), lambda t, meta: (0, meta[0] * tiles + t)),
+                pl.BlockSpec((depth, TILE), lambda t, side, *_: (0, (side[0] ^ mask) * tiles + t)),
             ],
             out_specs=pl.BlockSpec((rows, TILE), lambda t, *_: (0, t)),
         ),
@@ -242,17 +245,17 @@
         compiler_params=params(16),
         cost_estimate=cost(2 * rows * depth * block_width, depth * block_width * 2),
         name="up",
-    )(meta, packed, w_up)
-
-
-def down_kernel(meta, *refs, first):
+    )(side, packed, w_up)
+
+
+def down_kernel(side, *refs, first):
     a_ref, w_ref = refs[0], refs[1]
     out_ref = refs[-1]
     part = jnp.dot(a_ref[...], w_ref[...], preferred_element_type=f32)
     out_ref[...] = part if first else refs[2][...] + part
 
 
-def down(meta, active, w_down, before):
+def down(side, active, w_down, before, mask):
     rows, depth = active.shape
     width = w_down.shape[1]
     tile = 512
@@ -264,7 +267,7 @@
             grid=(width // tile,),
             in_specs=[
                 pl.BlockSpec((rows, depth), lambda t, *_: (0, 0)),
-                pl.BlockSpec((depth, tile), lambda t, meta: (meta[0], t)),
+                pl.BlockSpec((depth, tile), lambda t, side, *_: (side[0] ^ mask, t)),
             ]
             + ([] if before is None else [sums]),
             out_specs=sums,
@@ -273,10 +276,10 @@
         compiler_params=params(16),
         cost_estimate=cost(2 * rows * depth * width, depth * width * 2),
         name="down",
-    )(meta, active, w_down, *([] if before is None else [before]))
-
-
-def down_unpack_kernel(meta, a_ref, w_ref, before_ref, *outs):
+    )(side, active, w_down, *([] if before is None else [before]))
+
+
+def down_unpack_kernel(side, layout, a_ref, w_ref, before_ref, *outs):
     parts = len(outs)
     rows = a_ref.shape[0]
     pieces = outs[0].shape[0] // PAD
@@ -287,25 +290,25 @@
     for part in range(parts):
         picks = []
         for piece in range(pieces):
-            base = meta[1 + part * pieces + piece]
-            count = meta[1 + parts * pieces + part * pieces + piece]
+            base = layout[part * pieces + piece]
+            count = layout[(parts + part) * pieces + piece]
             picks.append(jnp.logical_and(column - row == base, row < count).astype(f32))
         pick = jnp.concatenate(picks, axis=0).astype(bf16)
         outs[part][...] = jnp.dot(pick, share, preferred_element_type=f32).astype(bf16)
 
 
-def down_unpack(meta, active, w_down, before, parts, per):
+def down_unpack(side, layout, active, w_down, before, parts, per, mask):
     rows, depth = active.shape
     width = w_down.shape[1]
     tile = 512
     return pl.pallas_call(
         down_unpack_kernel,
         grid_spec=pltpu.PrefetchScalarGridSpec(
-            num_scalar_prefetch=1,
+            num_scalar_prefetch=2,
             grid=(width // tile,),
             in_specs=[
                 pl.BlockSpec((rows, depth), lambda t, *_: (0, 0)),
-                pl.BlockSpec((depth, tile), lambda t, meta: (meta[0], t)),
+                pl.BlockSpec((depth, tile), lambda t, side, *_: (side[0] ^ mask, t)),
                 pl.BlockSpec((rows, tile), lambda t, *_: (0, t)),
             ],
             out_specs=[pl.BlockSpec((per, tile), lambda t, *_: (0, t))] * parts,
@@ -314,7 +317,7 @@
         compiler_params=params(16),
         cost_estimate=cost(2 * rows * depth * width, depth * width * 2),
         name="down_unpack",
-    )(meta, active, w_down, before)
+    )(side, layout, active, w_down, before)
 
 
 def finish_kernel(lengths, where_side, mixed_ref, *refs):
@@ -366,13 +369,13 @@
     return lax.optimization_barrier((x, *others))[0]
 
 
-def feed_forward(rows, meta_of, gathered, w_up, w_down):
+def feed_forward(rows, side, layout, gathered, w_up, w_down):
     width = w_up.shape[1] // 4
-    packed, far_partner = pack_up(meta_of(3), gathered, w_up, rows, width)
+    packed, far_partner = pack_up(side, layout, gathered, w_up, rows, width, 3)
     met = swap(far_partner, "side", 4, 1)
-    near = up(meta_of(1), packed, w_up, width, bf16)
-    far = up(meta_of(2), packed, w_up, width, bf16)
-    own = up(meta_of(0), packed, w_up, width, f32)
+    near = up(side, packed, w_up, width, bf16, 1)
+    far = up(side, packed, w_up, width, bf16, 2)
+    own = up(side, packed, w_up, width, f32, 0)
     pair_sum = added(far, met)
     crossed = swap(pair_sum, "side", 4, 2)
     near = swap(tie(near, met), "side", 4, 1)
@@ -382,19 +385,61 @@
     across = swap(active, "side", 4, 2)
     beside = swap(active, "side", 4, 1)
     forwarded = swap(across, "side", 4, 1)
-    total = down(meta_of(0), active, w_down, None)
-    total = down(meta_of(1), beside, w_down, total)
-    total = down(meta_of(2), across, w_down, total)
-    return down_unpack(meta_of(3), forwarded, w_down, total, len(gathered), gathered[0].shape[0])
+    total = down(side, active, w_down, None, 0)
+    total = down(side, beside, w_down, total, 1)
+    total = down(side, across, w_down, total, 2)
+    parts, per = len(gathered), gathered[0].shape[0]
+    return down_unpack(side, layout, forwarded, w_down, total, parts, per, 3)
+
+
+def layout_kernel(side, shard, *refs):
+    parts, out = refs[:-1], refs[-1]
+    pieces = parts[0].shape[0] // PAD
+    devices = len(parts) * pieces
+    counts, places = [], []
+    for part in range(len(parts)):
+        for piece in range(pieces):
+            last = parts[part][piece * PAD : (piece + 1) * PAD, :].astype(f32)[PAD - 1 :]
+            counts.append(jnp.max(last).astype(i32))
+            places.append(lax.rem(side[0] - piece + pieces, pieces) * len(parts) + (shard[0] ^ part))
+    total = jnp.int32(0)
+    for one in range(devices):
+        base = jnp.int32(0)
+        for other in range(devices):
+            base = base + jnp.where(places[other] < places[one], counts[other], 0)
+        out[one] = base
+        out[devices + one] = counts[one]
+        total = total + counts[one]
+    out[2 * devices] = total
+
+
+def read_layout(side, shard, gathered):
+    per = gathered[0].shape[0]
+    pieces = per // PAD
+    scalars = pl.BlockSpec(memory_space=pltpu.SMEM)
+    return pl.pallas_call(
+        layout_kernel,
+        grid=(1,),
+        in_specs=[scalars, scalars] + [pl.BlockSpec((per, 128), lambda t: (0, 0))] * len(gathered),
+        out_specs=scalars,
+        out_shape=jax.ShapeDtypeStruct((2 * len(gathered) * pieces + 1,), i32),
+        compiler_params=params(16),
+        name="layout",
+    )(side, shard, *gathered)
+
+
+ROW_STEPS = (96, 112, 128, 144, 160, 176, 192)
 
 
 def line_shards(
     queries, new_kv, kv_pool, page_table, ctx_len, residual_in, norm_gain, w_up, w_down
 ):
     i, s = lax.axis_index("side"), lax.axis_index("shard")
-    side = i.reshape(1)
-    count = jnp.sum((ctx_len > 0).astype(i32))
-    counts = lax.all_gather(count.reshape(1), ("side", "shard"), axis=0, tiled=True)
+    side, shard = i.reshape(1), s.reshape(1)
+    in_hbm = lambda x: pltpu.with_memory_space_constraint(x, pltpu.HBM)
+    queries, new_kv, kv_pool, residual_in, w_up, w_down = map(
+        in_hbm, (queries, new_kv, kv_pool, residual_in, w_up, w_down)
+    )
     mixed, *sends = attend(
         queries, new_kv, kv_pool, page_table, ctx_len, residual_in, norm_gain, side, 4
     )
@@ -405,16 +450,14 @@
     by_core = swap(here, "shard", 4, 1)
     by_both = swap(by_x, "shard", 4, 1)
     gathered = [here, by_core, by_x, by_both]
-
-    starts = jnp.cumsum(counts) - counts
-    order = jnp.stack([((i - shift) % 4) * 4 + (s ^ q) for q in range(4) for shift in range(4)])
-    layout = jnp.concatenate([starts[order], counts[order]])
-
-    def meta_of(mask):
-        return jnp.concatenate([(i ^ mask).reshape(1), layout]).astype(i32)
-
-    rows = 4 * 4 * LIVE_CAP
-    mine, for_core, for_x, for_both = feed_forward(rows, meta_of, gathered, w_up, w_down)
+    layout = read_layout(side, shard, gathered)
+    live = layout[-1]
+    step = sum((live > rows).astype(i32) for rows in ROW_STEPS[:-1])
+    mine, for_core, for_x, for_both = lax.switch(
+        step,
+        [functools.partial(feed_forward, rows) for rows in ROW_STEPS],
+        side, layout, gathered, w_up, w_down,
+    )
     back = swap(jnp.concatenate([for_core, for_both], axis=0), "shard", 4, 1)
     half = back.shape[0] // 2
     to_x = added(for_x, back[half:])

time: 140 us -> 116 us (0.83)
  local copies, waits for them, and re-layouts: 23.1 us -> 2.71 us
  blocking collectives: 10.3 us -> 0 us
  Pallas kernels: 34.4 us -> 43.5 us
  between operations: 0.24 us -> 3.98 us
  waiting for transfers between devices: 49.3 us -> 45.6 us
  starting transfers between devices: 20.6 us -> 18.8 us
    unnamed x34 -> x9, local copies, waits for them, and re-layouts: 20.8 us -> 1.37 us
    unnamed x1 -> x0, blocking collectives: 10.3 us -> none
    ppermute x11, waiting for transfers between devices: 40.5 us -> 36.7 us  [swap(): return lax.ppermute(x, axis, [(j, j ^ mask) for j in range(count)])]
    pallas_call x3, Pallas kernels: 7.91 us -> 10.8 us  [down(): pl.pallas_call(functools.partial(down_kernel, first=before is None), grid...]
    ppermute x11, starting transfers between devices: 10.1 us -> 7.87 us  [swap(): return lax.ppermute(x, axis, [(j, j ^ mask) for j in range(count)])]
    pallas_call x3, Pallas kernels: 8.53 us -> 10.6 us  [up(): pl.pallas_call(up_kernel, grid_spec=pltpu.PrefetchScalarGridSpec(num_scal...]
  transfers between devices with their start and end apart: 17 -> 17, of which waited for: 13 -> 13; matrix products, arithmetic and copies ran while one was open for 3% -> 0% of each run, Pallas kernels for 12% -> 19%
where the time goes in v2:
time: 116 us; the launch traced here: 115 us
  waiting for transfers between devices  45.6 us (39%)
  Pallas kernels  43.5 us (38%)
  starting transfers between devices  18.8 us (16%)
  between operations  3.98 us (3%)
  local copies, waits for them, and re-layouts  2.71 us (2%)
    ppermute x11, waiting for transfers between devices, swap(): return lax.ppermute(x, axis, [(j, j ^ mask) for j in range(count)])  36.7 us
    ppermute x6, starting transfers between devices, shifted(): lax.ppermute(x, axis, [(j, (j + shift) % count) for j in range(count)])  11 us
    pallas_call x3, Pallas kernels, down(): pl.pallas_call(functools.partial(down_kernel, first=before is None), grid...  10.8 us
    pallas_call x3, Pallas kernels, up(): pl.pallas_call(up_kernel, grid_spec=pltpu.PrefetchScalarGridSpec(num_scal...  10.6 us
    pallas_call x1, Pallas kernels, attend(): pl.pallas_call(attend_kernel, grid_spec=pltpu.PrefetchScalarGridSpec(num_...  9.89 us
    ppermute x6, waiting for transfers between devices, shifted(): lax.ppermute(x, axis, [(j, (j + shift) % count) for j in range(count)])  9 us
    ppermute x11, starting transfers between devices, swap(): return lax.ppermute(x, axis, [(j, j ^ mask) for j in range(count)])  7.87 us
    pallas_call x1, Pallas kernels, down_unpack(): pl.pallas_call(down_unpack_kernel, grid_spec=pltpu.PrefetchScalarGridSpec...  4.8 us
  transfers between devices with their start and end apart: 17, of which 13 were waited for; matrix products, arithmetic and copies ran while one was open for 0% of the time, Pallas kernels for 19%

profile of v2, /device:TPU:0, one launch (start us, length us, event | category | flops | bytes accessed | tf_op | source)
XLA Modules:
  0.0 115.5 jit_solution(13832166668912082799)
XLA Ops:
  0.0 0.7 reshape.42.gain_ref
  0.7 0.0 copy-start
  0.8 0.7 copy-done
  1.4 0.7 copy-done.1
  2.1 9.9 %attend.1 = (f32[15,8192]{1,0:T(8,128)S(1)}, bf16[16,2048]{1,0:T(8,128)(2,1)S(1)}, bf16[16,2048]{1,0:T(8,128)(2,1)S(1)}, bf16[16,2048]{1,0:T(8,128)(2,1)S(1)}, bf16[16,2048]{1,0:T(8,128)(2,1)S(1)}) custom-call(s32[15]{0:T(128)S(1)} %copy-done.1, s32[1]{0:T(128)} %bitcast.where_side.side, bf16[15,8192]{1,0:T(8,128)(2,1)} %q_ref.1, bf16[15,2048]{1,0:T(8,128)(2,1)} %nv_ref.1, ...), custom_call_target="tpu_custom_call" | custom-call | flops 939524096 | bytes 7340032 | tf_op jit(solution)/shard_map/attend/pallas_call | solution.py:141
  12.0 3.1 %collective-permute-start.42 = (bf16[16,2048]{1,0:T(8,128)(2,1)S(1)}, bf16[16,2048]{1,0:T(8,128)(2,1)S(1)}, u32[]{:S(2)}, u32[]{:S(2)}) collective-permute-start(bf16[16,2048]{1,0:T(8,128)(2,1)S(1)} %get-tuple-element.240), channel_id=1, source_target_pairs={{0,4},{4,8},{8,12},{12,0},{1,5},{5,9},{9,13},{13,1},{2,6},{6,10},{... | collective-permute-start | bytes 196616 | tf_op jit(solution)/shard_map/ppermute | solution.py:361
  15.1 2.6 %collective-permute-start.43 = (bf16[16,2048]{1,0:T(8,128)(2,1)S(1)}, bf16[16,2048]{1,0:T(8,128)(2,1)S(1)}, u32[]{:S(2)}, u32[]{:S(2)}) collective-permute-start(bf16[16,2048]{1,0:T(8,128)(2,1)S(1)} %get-tuple-element.241), channel_id=1, source_target_pairs={{0,8},{4,12},{8,0},{12,4},{1,9},{5,13},{9,1},{13,5},{2,10},{6,14},... | collective-permute-start | bytes 196616 | tf_op jit(solution)/shard_map/ppermute | solution.py:361
  17.7 1.3 %collective-permute-start.44 = (bf16[16,2048]{1,0:T(8,128)(2,1)S(1)}, bf16[16,2048]{1,0:T(8,128)(2,1)S(1)}, u32[]{:S(2)}, u32[]{:S(2)}) collective-permute-start(bf16[16,2048]{1,0:T(8,128)(2,1)S(1)} %get-tuple-element.242), channel_id=1, source_target_pairs={{0,12},{4,0},{8,4},{12,8},{1,13},{5,1},{9,5},{13,9},{2,14},{6,2},{... | collective-permute-start | bytes 196616 | tf_op jit(solution)/shard_map/ppermute | solution.py:361
  19.0 0.6 collective-permute-done.42
  19.6 2.5 %collective-permute-done.43 = bf16[16,2048]{1,0:T(8,128)(2,1)S(1)} collective-permute-done((bf16[16,2048]{1,0:T(8,128)(2,1)S(1)}, bf16[16,2048]{1,0:T(8,128)(2,1)S(1)}, u32[]{:S(2)}, u32[]{:S(2)}) %collective-permute-start.43) | collective-permute-done | bytes 65568 | tf_op jit(solution)/shard_map/ppermute | solution.py:361
  22.2 0.2 collective-permute-done.44
  22.4 1.6 %collective-permute-start.46 = (bf16[64,2048]{1,0:T(8,128)(2,1)S(1)}, bf16[64,2048]{1,0:T(8,128)(2,1)S(1)}, u32[]{:S(2)}, u32[]{:S(2)}) collective-permute-start(bf16[64,2048]{1,0:T(8,128)(2,1)S(1)} %constant_dynamic-update-slice_fusion.refs_0_), channel_id=1, source_target_pairs={{0,2},{1,3},{2,0},{3,1},{4,6},{5,7},{6,4},{7,5},{8,10},{9,11},{10,... | collective-permute-start | bytes 786440 | tf_op jit(solution)/shard_map/ppermute | solution.py:357
  24.0 6.3 %collective-permute-done.46.refs_2_ = bf16[64,2048]{1,0:T(8,128)(2,1)S(1)} collective-permute-done((bf16[64,2048]{1,0:T(8,128)(2,1)S(1)}, bf16[64,2048]{1,0:T(8,128)(2,1)S(1)}, u32[]{:S(2)}, u32[]{:S(2)}) %collective-permute-start.46) | collective-permute-done | bytes 262176 | tf_op jit(solution)/shard_map/ppermute | solution.py:357
  30.3 1.5 %collective-permute-done.47.refs_3_ = bf16[64,2048]{1,0:T(8,128)(2,1)S(1)} collective-permute-done((bf16[64,2048]{1,0:T(8,128)(2,1)S(1)}, bf16[64,2048]{1,0:T(8,128)(2,1)S(1)}, u32[]{:S(2)}, u32[]{:S(2)}) %collective-permute-start.47) | collective-permute-done | bytes 262176 | tf_op jit(solution)/shard_map/ppermute | solution.py:357
  31.8 1.2 layout.1
  33.0 0.6 slice.25
  37.4 56.3 %conditional.1 = ((bf16[64,2048]{1,0:T(8,128)(2,1)S(1)}, bf16[64,2048]{1,0:T(8,128)(2,1)S(1)}, bf16[64,2048]{1,0:T(8,128)(2,1)S(1)}, bf16[64,2048]{1,0:T(8,128)(2,1)S(1)})) conditional(s32[]{:T(128)} %bitcast.2, (s32[1]{0:T(128)}, s32[33]{0:T(128)S(1)}, bf16[64,2048]{1,0:T(8,128)(2,1)S(1)}, ...), branch_computations={%region_0.0_spmd, %region_1.0_spmd, %region_2.0_spmd, %region_3.0_... | conditional | flops 6444613632 | bytes 46137592 | solution.py:456
  37.5 4.8 %pack_up.9 = (bf16[128,2048]{1,0:T(8,128)(2,1)S(1)}, bf16[128,1024]{1,0:T(8,128)(2,1)S(1)}) custom-call(s32[1]{0:T(128)} %get-tuple-element.174.side, s32[33]{0:T(128)S(1)} %get-tuple-element.175.layout, bf16[64,2048]{1,0:T(8,128)(2,1)S(1)} %get-tuple-element.176.refs_0_, bf16[64,2048]{1,0:T(8,128)(2,1)S(1)} %get-tuple-element.177.refs_1_, ...), custom_call_target="tpu_custom_call" | custom-call | flops 536870912 | bytes 4194304 | tf_op jit(solution)/shard_map/cond/branch_2_fun/pack_up/pallas_call | solution.py:208
  42.3 1.9 %collective-permute-start.12 = (bf16[128,1024]{1,0:T(8,128)(2,1)S(1)}, bf16[128,1024]{1,0:T(8,128)(2,1)S(1)}, u32[]{:S(2)}, u32[]{:S(2)}) collective-permute-start(bf16[128,1024]{1,0:T(8,128)(2,1)S(1)} %get-tuple-element.182), channel_id=1, source_target_pairs={{0,4},{4,0},{8,12},{12,8},{1,5},{5,1},{9,13},{13,9},{2,6},{6,2},{1... | collective-permute-start | bytes 786440 | tf_op jit(solution)/shard_map/cond/branch_2_fun/ppermute | solution.py:357
  44.2 3.5 %up.28 = bf16[128,1024]{1,0:T(8,128)(2,1)S(1)} custom-call(s32[1]{0:T(128)} %get-tuple-element.174.side, bf16[128,2048]{1,0:T(8,128)(2,1)S(1)} %get-tuple-element.181.x_ref, bf16[2048,4096]{1,0:T(8,128)(2,1)} %get-tuple-element.180.refs_4_.w_ref), custom_call_target="tpu_custom_call" | custom-call | flops 536870912 | bytes 4194304 | tf_op jit(solution)/shard_map/cond/branch_2_fun/up/pallas_call | solution.py:233
  47.8 3.6 %up.29 = bf16[128,1024]{1,0:T(8,128)(2,1)S(1)} custom-call(s32[1]{0:T(128)} %get-tuple-element.174.side, bf16[128,2048]{1,0:T(8,128)(2,1)S(1)} %get-tuple-element.181.x_ref, bf16[2048,4096]{1,0:T(8,128)(2,1)} %get-tuple-element.180.refs_4_.w_ref), custom_call_target="tpu_custom_call" | custom-call | flops 536870912 | bytes 4194304 | tf_op jit(solution)/shard_map/cond/branch_2_fun/up/pallas_call | solution.py:233
  51.3 1.2 %collective-permute-start.13 = (bf16[128,1024]{1,0:T(8,128)(2,1)S(1)}, bf16[128,1024]{1,0:T(8,128)(2,1)S(1)}, u32[]{:S(2)}, u32[]{:S(2)}) collective-permute-start(bf16[128,1024]{1,0:T(8,128)(2,1)S(1)} %up.28), channel_id=1, source_target_pairs={{0,4},{4,0},{8,12},{12,8},{1,5},{5,1},{9,13},{13,9},{2,6},{6,2},{1... | collective-permute-start | bytes 786440 | tf_op jit(solution)/shard_map/cond/branch_2_fun/ppermute | solution.py:357
  52.6 0.1 add_convert_fusion.2
  52.6 0.4 collective-permute-start.14
  53.0 3.5 %up.27 = f32[128,1024]{1,0:T(8,128)S(1)} custom-call(s32[1]{0:T(128)} %get-tuple-element.174.side, bf16[128,2048]{1,0:T(8,128)(2,1)S(1)} %get-tuple-element.181.x_ref, bf16[2048,4096]{1,0:T(8,128)(2,1)} %get-tuple-element.180.refs_4_.w_ref), custom_call_target="tpu_custom_call" | custom-call | flops 536870912 | bytes 4194304 | tf_op jit(solution)/shard_map/cond/branch_2_fun/up/pallas_call | solution.py:233
  56.5 7.0 %collective-permute-done.13 = bf16[128,1024]{1,0:T(8,128)(2,1)S(1)} collective-permute-done((bf16[128,1024]{1,0:T(8,128)(2,1)S(1)}, bf16[128,1024]{1,0:T(8,128)(2,1)S(1)}, u32[]{:S(2)}, u32[]{:S(2)}) %collective-permute-start.13) | collective-permute-done | bytes 262176 | tf_op jit(solution)/shard_map/cond/branch_2_fun/ppermute | solution.py:357
  63.5 3.3 %collective-permute-done.14 = bf16[128,1024]{1,0:T(8,128)(2,1)S(1)} collective-permute-done((bf16[128,1024]{1,0:T(8,128)(2,1)S(1)}, bf16[128,1024]{1,0:T(8,128)(2,1)S(1)}, u32[]{:S(2)}, u32[]{:S(2)}) %collective-permute-start.14) | collective-permute-done | bytes 262176 | tf_op jit(solution)/shard_map/cond/branch_2_fun/ppermute | solution.py:357
  66.8 0.1 multiply_convert_fusion.2.refs_0_
  66.9 0.1 collective-permute-start.15
  67.0 1.4 %collective-permute-start.17 = (bf16[128,1024]{1,0:T(8,128)(2,1)S(1)}, bf16[128,1024]{1,0:T(8,128)(2,1)S(1)}, u32[]{:S(2)}, u32[]{:S(2)}) collective-permute-start(bf16[128,1024]{1,0:T(8,128)(2,1)S(1)} %multiply_convert_fusion.2.refs_0_), channel_id=1, source_target_pairs={{0,4},{4,0},{8,12},{12,8},{1,5},{5,1},{9,13},{13,9},{2,6},{6,2},{1... | collective-permute-start | bytes 786440 | tf_op jit(solution)/shard_map/cond/branch_2_fun/ppermute | solution.py:357
  68.4 9.5 %collective-permute-done.15.refs_0_ = bf16[128,1024]{1,0:T(8,128)(2,1)S(1)} collective-permute-done((bf16[128,1024]{1,0:T(8,128)(2,1)S(1)}, bf16[128,1024]{1,0:T(8,128)(2,1)S(1)}, u32[]{:S(2)}, u32[]{:S(2)}) %collective-permute-start.15) | collective-permute-done | bytes 262176 | tf_op jit(solution)/shard_map/cond/branch_2_fun/ppermute | solution.py:357
  77.9 3.6 %down.27.refs_2_ = f32[128,2048]{1,0:T(8,128)S(1)} custom-call(s32[1]{0:T(128)} %get-tuple-element.174.side, bf16[128,1024]{1,0:T(8,128)(2,1)S(1)} %multiply_convert_fusion.2.refs_0_, bf16[4096,2048]{1,0:T(8,128)(2,1)} %get-tuple-element.184.refs_1_.w_ref), custom_call_target="tpu_custom_call" | custom-call | flops 536870912 | bytes 4194304 | tf_op jit(solution)/shard_map/cond/branch_2_fun/down/pallas_call | solution.py:263
  81.4 3.6 %down.28.refs_2_ = f32[128,2048]{1,0:T(8,128)S(1)} custom-call(s32[1]{0:T(128)} %get-tuple-element.174.side, bf16[128,1024]{1,0:T(8,128)(2,1)S(1)} %collective-permute-done.17.refs_0_, bf16[4096,2048]{1,0:T(8,128)(2,1)} %get-tuple-element.184.refs_1_.w_ref, f32[128,2048]{1,0:T(8,128)S(1)} %down.27.refs_2_), custom_call_target="tpu_custom_call" | custom-call | flops 536870912 | bytes 4194304 | tf_op jit(solution)/shard_map/cond/branch_2_fun/down/pallas_call | solution.py:263
  85.1 3.6 %down.29.before_ref = f32[128,2048]{1,0:T(8,128)S(1)} custom-call(s32[1]{0:T(128)} %get-tuple-element.174.side, bf16[128,1024]{1,0:T(8,128)(2,1)S(1)} %collective-permute-done.15.refs_0_, bf16[4096,2048]{1,0:T(8,128)(2,1)} %get-tuple-element.184.refs_1_.w_ref, f32[128,2048]{1,0:T(8,128)S(1)} %down.28.refs_2_), custom_call_target="tpu_custom_call" | custom-call | flops 536870912 | bytes 4194304 | tf_op jit(solution)/shard_map/cond/branch_2_fun/down/pallas_call | solution.py:263
  88.7 4.8 %down_unpack.9 = (bf16[64,2048]{1,0:T(8,128)(2,1)S(1)}, bf16[64,2048]{1,0:T(8,128)(2,1)S(1)}, bf16[64,2048]{1,0:T(8,128)(2,1)S(1)}, bf16[64,2048]{1,0:T(8,128)(2,1)S(1)}) custom-call(s32[1]{0:T(128)} %get-tuple-element.174.side, s32[33]{0:T(128)S(1)} %get-tuple-element.175.layout, bf16[128,1024]{1,0:T(8,128)(2,1)S(1)} %collective-permute-done.16.a_ref, ...), custom_call_target="tpu_custom_call" | custom-call | flops 536870912 | bytes 4194304 | tf_op jit(solution)/shard_map/cond/branch_2_fun/down_unpack/pallas_call | solution.py:304
  93.8 0.1 collective-permute-start.48
  93.9 1.9 %collective-permute-done.48 = bf16[128,2048]{1,0:T(8,128)(2,1)S(1)} collective-permute-done((bf16[128,2048]{1,0:T(8,128)(2,1)S(1)}, bf16[128,2048]{1,0:T(8,128)(2,1)S(1)}, u32[]{:S(2)}, u32[]{:S(2)}) %collective-permute-start.48) | collective-permute-done | bytes 524320 | tf_op jit(solution)/shard_map/ppermute | solution.py:357
  95.8 0.1 fusion.1
  95.9 1.1 collective-permute-start.49
  97.0 7.3 %collective-permute-done.49 = bf16[64,2048]{1,0:T(8,128)(2,1)S(1)} collective-permute-done((bf16[64,2048]{1,0:T(8,128)(2,1)S(1)}, bf16[64,2048]{1,0:T(8,128)(2,1)S(1)}, u32[]{:S(2)}, u32[]{:S(2)}) %collective-permute-start.49) | collective-permute-done | bytes 262176 | tf_op jit(solution)/shard_map/ppermute | solution.py:357
  104.3 0.1 add_convert_fusion.7
  104.4 1.4 %collective-permute-start.50 = (bf16[16,2048]{1,0:T(8,128)(2,1)S(1)}, bf16[16,2048]{1,0:T(8,128)(2,1)S(1)}, u32[]{:S(2)}, u32[]{:S(2)}) collective-permute-start(bf16[16,2048]{1,0:T(8,128)(2,1)S(1)} %get-tuple-element.284), channel_id=1, source_target_pairs={{0,12},{4,0},{8,4},{12,8},{1,13},{5,1},{9,5},{13,9},{2,14},{6,2},{... | collective-permute-start | bytes 196616 | tf_op jit(solution)/shard_map/ppermute | solution.py:361
  105.8 2.2 %collective-permute-start.51 = (bf16[16,2048]{1,0:T(8,128)(2,1)S(1)}, bf16[16,2048]{1,0:T(8,128)(2,1)S(1)}, u32[]{:S(2)}, u32[]{:S(2)}) collective-permute-start(bf16[16,2048]{1,0:T(8,128)(2,1)S(1)} %get-tuple-element.283), channel_id=1, source_target_pairs={{0,8},{4,12},{8,0},{12,4},{1,9},{5,13},{9,1},{13,5},{2,10},{6,14},... | collective-permute-start | bytes 196616 | tf_op jit(solution)/shard_map/ppermute | solution.py:361
  108.0 0.4 collective-permute-start.52
  108.4 0.7 collective-permute-done.50.refs_1_
  109.1 3.6 %collective-permute-done.51.refs_2_ = bf16[16,2048]{1,0:T(8,128)(2,1)S(1)} collective-permute-done((bf16[16,2048]{1,0:T(8,128)(2,1)S(1)}, bf16[16,2048]{1,0:T(8,128)(2,1)S(1)}, u32[]{:S(2)}, u32[]{:S(2)}) %collective-permute-start.51) | collective-permute-done | bytes 65568 | tf_op jit(solution)/shard_map/ppermute | solution.py:361
  112.7 1.3 %collective-permute-done.52.refs_3_ = bf16[16,2048]{1,0:T(8,128)(2,1)S(1)} collective-permute-done((bf16[16,2048]{1,0:T(8,128)(2,1)S(1)}, bf16[16,2048]{1,0:T(8,128)(2,1)S(1)}, u32[]{:S(2)}, u32[]{:S(2)}) %collective-permute-start.52) | collective-permute-done | bytes 65568 | tf_op jit(solution)/shard_map/ppermute | solution.py:361
  114.0 1.5 %finish.1 = bf16[15,8192]{1,0:T(8,128)(2,1)} custom-call(s32[15]{0:T(128)S(1)} %copy-done.2, s32[1]{0:T(128)} %bitcast.where_side.side, f32[15,8192]{1,0:T(8,128)S(1)} %get-tuple-element.238.mixed_ref, bf16[16,2048]{1,0:T(8,128)(2,1)S(1)} %get-tuple-element.285.refs_0_, bf16[16,2048]{1,0:T(8,128)(2,1)S(1)} %collective-permute-done.50.refs_1_, ...), custom_call_target="tpu_custom_call" | custom-call | flops 3932160 | bytes 983040 | tf_op jit(solution)/shard_map/finish/pallas_call | solution.py:345
  (16 shorter events, 0.1 us)
Async XLA Ops:
  0.7 0.7 copy-start
  1.4 0.7 copy-start.1
  12.0 7.6 %collective-permute-start.42 = (bf16[16,2048]{1,0:T(8,128)(2,1)S(1)}, bf16[16,2048]{1,0:T(8,128)(2,1)S(1)}, u32[]{:S(2)}, u32[]{:S(2)}) collective-permute-start(bf16[16,2048]{1,0:T(8,128)(2,1)S(1)} %get-tuple-element.240), channel_id=1, source_target_pairs={{0,4},{4,8},{8,12},{12,0},{1,5},{5,9},{9,13},{13,1},{2,6},{6,10},{... | collective-permute-start | bytes 196616 | tf_op jit(solution)/shard_map/ppermute | solution.py:361
  15.1 7.1 %collective-permute-start.43 = (bf16[16,2048]{1,0:T(8,128)(2,1)S(1)}, bf16[16,2048]{1,0:T(8,128)(2,1)S(1)}, u32[]{:S(2)}, u32[]{:S(2)}) collective-permute-start(bf16[16,2048]{1,0:T(8,128)(2,1)S(1)} %get-tuple-element.241), channel_id=1, source_target_pairs={{0,8},{4,12},{8,0},{12,4},{1,9},{5,13},{9,1},{13,5},{2,10},{6,14},... | collective-permute-start | bytes 196616 | tf_op jit(solution)/shard_map/ppermute | solution.py:361
  17.7 4.7 %collective-permute-start.44 = (bf16[16,2048]{1,0:T(8,128)(2,1)S(1)}, bf16[16,2048]{1,0:T(8,128)(2,1)S(1)}, u32[]{:S(2)}, u32[]{:S(2)}) collective-permute-start(bf16[16,2048]{1,0:T(8,128)(2,1)S(1)} %get-tuple-element.242), channel_id=1, source_target_pairs={{0,12},{4,0},{8,4},{12,8},{1,13},{5,1},{9,5},{13,9},{2,14},{6,2},{... | collective-permute-start | bytes 196616 | tf_op jit(solution)/shard_map/ppermute | solution.py:361
  22.4 7.9 %collective-permute-start.46 = (bf16[64,2048]{1,0:T(8,128)(2,1)S(1)}, bf16[64,2048]{1,0:T(8,128)(2,1)S(1)}, u32[]{:S(2)}, u32[]{:S(2)}) collective-permute-start(bf16[64,2048]{1,0:T(8,128)(2,1)S(1)} %constant_dynamic-update-slice_fusion.refs_0_), channel_id=1, source_target_pairs={{0,2},{1,3},{2,0},{3,1},{4,6},{5,7},{6,4},{7,5},{8,10},{9,11},{10,... | collective-permute-start | bytes 786440 | tf_op jit(solution)/shard_map/ppermute | solution.py:357
  24.0 6.3 %collective-permute-start.45 = (bf16[64,2048]{1,0:T(8,128)(2,1)S(1)}, bf16[64,2048]{1,0:T(8,128)(2,1)S(1)}, u32[]{:S(2)}, u32[]{:S(2)}) collective-permute-start(bf16[64,2048]{1,0:T(8,128)(2,1)S(1)} %constant_dynamic-update-slice_fusion.refs_0_), channel_id=1, source_target_pairs={{0,1},{1,0},{2,3},{3,2},{4,5},{5,4},{6,7},{7,6},{8,9},{9,8},{10,11... | collective-permute-start | bytes 786440 | tf_op jit(solution)/shard_map/ppermute | solution.py:357
  30.3 1.5 %collective-permute-start.47 = (bf16[64,2048]{1,0:T(8,128)(2,1)S(1)}, bf16[64,2048]{1,0:T(8,128)(2,1)S(1)}, u32[]{:S(2)}, u32[]{:S(2)}) collective-permute-start(bf16[64,2048]{1,0:T(8,128)(2,1)S(1)} %collective-permute-done.46.refs_2_), channel_id=1, source_target_pairs={{0,1},{1,0},{2,3},{3,2},{4,5},{5,4},{6,7},{7,6},{8,9},{9,8},{10,11... | collective-permute-start | bytes 786440 | tf_op jit(solution)/shard_map/ppermute | solution.py:357
  42.3 9.0 %collective-permute-start.12 = (bf16[128,1024]{1,0:T(8,128)(2,1)S(1)}, bf16[128,1024]{1,0:T(8,128)(2,1)S(1)}, u32[]{:S(2)}, u32[]{:S(2)}) collective-permute-start(bf16[128,1024]{1,0:T(8,128)(2,1)S(1)} %get-tuple-element.182), channel_id=1, source_target_pairs={{0,4},{4,0},{8,12},{12,8},{1,5},{5,1},{9,13},{13,9},{2,6},{6,2},{1... | collective-permute-start | bytes 786440 | tf_op jit(solution)/shard_map/cond/branch_2_fun/ppermute | solution.py:357
  51.3 12.2 %collective-permute-start.13 = (bf16[128,1024]{1,0:T(8,128)(2,1)S(1)}, bf16[128,1024]{1,0:T(8,128)(2,1)S(1)}, u32[]{:S(2)}, u32[]{:S(2)}) collective-permute-start(bf16[128,1024]{1,0:T(8,128)(2,1)S(1)} %up.28), channel_id=1, source_target_pairs={{0,4},{4,0},{8,12},{12,8},{1,5},{5,1},{9,13},{13,9},{2,6},{6,2},{1... | collective-permute-start | bytes 786440 | tf_op jit(solution)/shard_map/cond/branch_2_fun/ppermute | solution.py:357
  52.6 14.1 %collective-permute-start.14 = (bf16[128,1024]{1,0:T(8,128)(2,1)S(1)}, bf16[128,1024]{1,0:T(8,128)(2,1)S(1)}, u32[]{:S(2)}, u32[]{:S(2)}) collective-permute-start(bf16[128,1024]{1,0:T(8,128)(2,1)S(1)} %add_convert_fusion.2), channel_id=1, source_target_pairs={{0,8},{4,12},{8,0},{12,4},{1,9},{5,13},{9,1},{13,5},{2,10},{6,14},... | collective-permute-start | bytes 786440 | tf_op jit(solution)/shard_map/cond/branch_2_fun/ppermute | solution.py:357
  66.9 11.0 %collective-permute-start.15 = (bf16[128,1024]{1,0:T(8,128)(2,1)S(1)}, bf16[128,1024]{1,0:T(8,128)(2,1)S(1)}, u32[]{:S(2)}, u32[]{:S(2)}) collective-permute-start(bf16[128,1024]{1,0:T(8,128)(2,1)S(1)} %multiply_convert_fusion.2.refs_0_), channel_id=1, source_target_pairs={{0,8},{4,12},{8,0},{12,4},{1,9},{5,13},{9,1},{13,5},{2,10},{6,14},... | collective-permute-start | bytes 786440 | tf_op jit(solution)/shard_map/cond/branch_2_fun/ppermute | solution.py:357
  67.0 14.4 %collective-permute-start.17 = (bf16[128,1024]{1,0:T(8,128)(2,1)S(1)}, bf16[128,1024]{1,0:T(8,128)(2,1)S(1)}, u32[]{:S(2)}, u32[]{:S(2)}) collective-permute-start(bf16[128,1024]{1,0:T(8,128)(2,1)S(1)} %multiply_convert_fusion.2.refs_0_), channel_id=1, source_target_pairs={{0,4},{4,0},{8,12},{12,8},{1,5},{5,1},{9,13},{13,9},{2,6},{6,2},{1... | collective-permute-start | bytes 786440 | tf_op jit(solution)/shard_map/cond/branch_2_fun/ppermute | solution.py:357
  77.9 10.8 %collective-permute-start.16 = (bf16[128,1024]{1,0:T(8,128)(2,1)S(1)}, bf16[128,1024]{1,0:T(8,128)(2,1)S(1)}, u32[]{:S(2)}, u32[]{:S(2)}) collective-permute-start(bf16[128,1024]{1,0:T(8,128)(2,1)S(1)} %collective-permute-done.15.refs_0_), channel_id=1, source_target_pairs={{0,4},{4,0},{8,12},{12,8},{1,5},{5,1},{9,13},{13,9},{2,6},{6,2},{1... | collective-permute-start | bytes 786440 | tf_op jit(solution)/shard_map/cond/branch_2_fun/ppermute | solution.py:357
  93.8 20.2 %copy-start.2 = (s32[15]{0:T(128)S(1)}, s32[15]{0:T(128)}, u32[]{:S(2)}) copy-start(s32[15]{0:T(128)} %lengths.3) | copy-start | bytes 184
  93.8 2.0 %collective-permute-start.48 = (bf16[128,2048]{1,0:T(8,128)(2,1)S(1)}, bf16[128,2048]{1,0:T(8,128)(2,1)S(1)}, u32[]{:S(2)}, u32[]{:S(2)}) collective-permute-start(bf16[128,2048]{1,0:T(8,128)(2,1)S(1)} %pad_maximum_fusion), channel_id=1, source_target_pairs={{0,1},{1,0},{2,3},{3,2},{4,5},{5,4},{6,7},{7,6},{8,9},{9,8},{10,11... | collective-permute-start | bytes 1572872 | tf_op jit(solution)/shard_map/ppermute | solution.py:357
  95.9 8.4 %collective-permute-start.49 = (bf16[64,2048]{1,0:T(8,128)(2,1)S(1)}, bf16[64,2048]{1,0:T(8,128)(2,1)S(1)}, u32[]{:S(2)}, u32[]{:S(2)}) collective-permute-start(bf16[64,2048]{1,0:T(8,128)(2,1)S(1)} %fusion.1), channel_id=1, source_target_pairs={{0,2},{1,3},{2,0},{3,1},{4,6},{5,7},{6,4},{7,5},{8,10},{9,11},{10,... | collective-permute-start | bytes 786440 | tf_op jit(solution)/shard_map/ppermute | solution.py:357
  104.4 4.7 %collective-permute-start.50 = (bf16[16,2048]{1,0:T(8,128)(2,1)S(1)}, bf16[16,2048]{1,0:T(8,128)(2,1)S(1)}, u32[]{:S(2)}, u32[]{:S(2)}) collective-permute-start(bf16[16,2048]{1,0:T(8,128)(2,1)S(1)} %get-tuple-element.284), channel_id=1, source_target_pairs={{0,12},{4,0},{8,4},{12,8},{1,13},{5,1},{9,5},{13,9},{2,14},{6,2},{... | collective-permute-start | bytes 196616 | tf_op jit(solution)/shard_map/ppermute | solution.py:361
  105.8 7.0 %collective-permute-start.51 = (bf16[16,2048]{1,0:T(8,128)(2,1)S(1)}, bf16[16,2048]{1,0:T(8,128)(2,1)S(1)}, u32[]{:S(2)}, u32[]{:S(2)}) collective-permute-start(bf16[16,2048]{1,0:T(8,128)(2,1)S(1)} %get-tuple-element.283), channel_id=1, source_target_pairs={{0,8},{4,12},{8,0},{12,4},{1,9},{5,13},{9,1},{13,5},{2,10},{6,14},... | collective-permute-start | bytes 196616 | tf_op jit(solution)/shard_map/ppermute | solution.py:361
  108.0 6.1 %collective-permute-start.52 = (bf16[16,2048]{1,0:T(8,128)(2,1)S(1)}, bf16[16,2048]{1,0:T(8,128)(2,1)S(1)}, u32[]{:S(2)}, u32[]{:S(2)}) collective-permute-start(bf16[16,2048]{1,0:T(8,128)(2,1)S(1)} %get-tuple-element.282), channel_id=1, source_target_pairs={{0,4},{4,8},{8,12},{12,0},{1,5},{5,9},{9,13},{13,1},{2,6},{6,10},{... | collective-permute-start | bytes 196616 | tf_op jit(solution)/shard_map/ppermute | solution.py:361

commit v3 on v0

v3 whole, which is shorter than its diff:
```python
import functools
import math

import jax
import jax.numpy as jnp
from jax import lax
from jax.experimental import pallas as pl
from jax.experimental.pallas import tpu as pltpu
from jax.sharding import PartitionSpec as P

KV_HEADS = 8
HEAD = 128
GROUP = 8
LIVE_CAP = 12
PAD = 16

epsilon = 1e-05
bf16, f32, i32 = jnp.bfloat16, jnp.float32, jnp.int32
VMEM_MB = 1 << 20


def params(mb, **more):
    return pltpu.CompilerParams(vmem_limit_bytes=mb * VMEM_MB, **more)


def cost(flops, bytes_accessed):
    return pl.CostEstimate(flops=int(flops), bytes_accessed=int(bytes_accessed), transcendentals=0)


def pad_rows(x):
    rows = x.shape[0]
    if rows == PAD:
        return x
    return jnp.concatenate([x, jnp.zeros((PAD - rows,) + x.shape[1:], x.dtype)], axis=0)


def live_ranks(lengths, slots):
    live, rank, count = [], [], jnp.int32(0)
    for slot in range(slots):
        alive = lengths[slot] > 0
        live.append(alive)
        rank.append(count)
        count = count + alive.astype(i32)
    return live, rank


def token_bias(lengths, table, pages, page):
    slots, entries = table.shape
    tokens = pages * page
    lanes = 128 * ((pages + 127) // 128)
    row = lax.broadcasted_iota(i32, (PAD, lanes), 0)
    column = lax.broadcasted_iota(i32, (PAD, lanes), 1)
    reach = jnp.zeros((PAD, lanes), i32)
    for slot in range(slots):
        reach = jnp.where(row == slot, lengths[slot], reach)
    table = pad_rows(table)
    seen = jnp.zeros((PAD, lanes), i32)
    for entry in range(entries):
        here = jnp.minimum(jnp.maximum(reach - entry * page, 0), page)
        seen = seen + jnp.where(table[:, entry : entry + 1] == column, here, 0)
    spread = (
        lax.broadcasted_iota(i32, (lanes, tokens), 1) // page
        == lax.broadcasted_iota(i32, (lanes, tokens), 0)
    )
    seen_tokens = jnp.dot(
        seen.astype(f32).astype(bf16), spread.astype(f32).astype(bf16), preferred_element_type=f32
    )
    place = (lax.broadcasted_iota(i32, (PAD, tokens), 1) % page).astype(f32)
    return jnp.where(place < seen_tokens, 0.0, -1e30)


def live_pick(lengths, slots, rows, offset, to_slots):
    live, rank = live_ranks(lengths, slots)
    shape = (PAD, rows) if to_slots else (rows, PAD)
    of_slot = lax.broadcasted_iota(i32, shape, 0 if to_slots else 1)
    of_rank = lax.broadcasted_iota(i32, shape, 1 if to_slots else 0) - offset
    pick = jnp.zeros(shape, f32)
    for slot in range(slots):
        chosen = jnp.logical_and(of_rank == rank[slot], of_slot == slot)
        pick = jnp.where(jnp.logical_and(chosen, live[slot]), 1.0, pick)
    return pick.astype(bf16), rank[-1] + live[-1].astype(i32)


SHIFTS = (2, 1, 3, 0)
POOL_CUTS = 4


def attend_kernel(lengths, side, *refs, sides, shift, following, first):
    last = following is None
    refs = list(refs)
    take = lambda n: [refs.pop(0) for _ in range(n)]
    if first:
        table_ref = refs.pop(0)
        sources = take(4)
        pool_ref = refs.pop(0)
    else:
        q_ref, new_ref, res_ref, gain_ref, bias_ref, k_ref, v_ref = take(7)
        pool_ref = None if last else refs.pop(0)
    send_ref, mixed_ref, square_ref = take(3)
    if first:
        q_ref, new_ref, res_ref, gain_ref, bias_ref = take(5)
    if not last:
        next_k_ref, next_v_ref = take(2)
    if first:
        k_ref, v_ref, gain_copy, sems, own_sems = take(5)
    if not last:
        next_sems = refs.pop(0)
    slots, step = mixed_ref.shape
    pages, page, columns = k_ref.shape
    heads = columns // HEAD
    tokens = pages * page
    cut = pages // POOL_CUTS
    scale = math.log2(math.e) / math.sqrt(HEAD)

    def fetch(target_k, target_v, towards, sems):
        block = lax.rem(side[0] + towards, sides)
        copies = []
        for target, at, row in ((target_k, block, 0), (target_v, sides + block, 1)):
            at = pl.multiple_of(at * columns, columns)
            for c in range(POOL_CUTS):
                rows = pl.ds(c * cut, cut)
                copy = pltpu.make_async_copy(
                    pool_ref.at[rows, :, pl.ds(at, columns)], target.at[rows], sems.at[row, c]
                )
                copy.start()
                copies.append(copy)
        return copies

    if first:
        small = [
            pltpu.make_async_copy(source, target, own_sems.at[n])
            for n, (source, target) in enumerate(
                zip(sources, (q_ref, new_ref, res_ref, gain_copy), strict=True)
            )
        ]
        for copy in small[:2]:
            copy.start()
        now = fetch(k_ref, v_ref, shift, sems)
        for copy in small[2:]:
            copy.start()
        ahead = fetch(next_k_ref, next_v_ref, following, next_sems)
        bias_ref[...] = token_bias(lengths, table_ref[...], pages, page)
        for copy in small + now:
            copy.wait()
        gain_ref[...] = gain_copy[...].astype(f32)
    elif not last:
        ahead = fetch(next_k_ref, next_v_ref, following, next_sems)

    block = lax.rem(side[0] + shift, sides)
    start = pl.multiple_of(block * step, step)
    new_start = pl.multiple_of(block * columns, columns)
    pick, count = live_pick(lengths, slots, PAD, 0, False)
    squares = jnp.zeros((slots, HEAD), f32)
    bias = bias_ref[...][None]
    for head in range(heads):
        across = slice(head * HEAD, (head + 1) * HEAD)
        base = head * GROUP * HEAD
        q = jnp.concatenate(
            [pad_rows(q_ref[:, pl.ds(start + base + g * HEAD, HEAD)]) for g in range(GROUP)],
            axis=0,
        )
        keys = k_ref[:, :, across].reshape(tokens, HEAD)
        values = v_ref[:, :, across].reshape(tokens, HEAD)
        new_at = new_start + head * HEAD
        new_key = pad_rows(new_ref[:, pl.ds(new_at, HEAD)]).astype(f32)
        new_value = pad_rows(new_ref[:, pl.ds(sides * columns + new_at, HEAD)]).astype(f32)
        scores = lax.dot_general(q, keys, (((1,), (1,)), ((), ())), preferred_element_type=f32)
        scores = scores.reshape(GROUP, PAD, tokens) * scale + bias
        own = jnp.sum(
            q.astype(f32).reshape(GROUP, PAD, HEAD) * new_key[None], axis=-1, keepdims=True
        )
        own = own * scale
        highest = jnp.maximum(jnp.max(scores, axis=-1, keepdims=True), own)
        weights = jnp.exp2(scores - highest)
        own_weight = jnp.exp2(own - highest)
        total = jnp.sum(weights, axis=-1, keepdims=True) + own_weight
        summed = jnp.dot(
            weights.astype(bf16).reshape(GROUP * PAD, tokens), values, preferred_element_type=f32
        ).reshape(GROUP, PAD, HEAD)
        attended = (summed + own_weight * new_value[None]) / total
        for g in range(GROUP):
            at = slice(base + g * HEAD, base + (g + 1) * HEAD)
            residual = res_ref[:, pl.ds(start + base + g * HEAD, HEAD)].astype(f32)
            mixed = residual + attended[g][:slots]
            mixed_ref[:, at] = mixed
            squares = squares + mixed * mixed
            gain = gain_ref[pl.ds(block * (step // HEAD) + head * GROUP + g, 1), :]
            gained = pad_rows((mixed * gain).astype(bf16))
            rows = jnp.dot(pick, gained, preferred_element_type=f32)
            counted = lax.broadcasted_iota(i32, rows.shape, 0) == PAD - 1
            send_ref[:, at] = jnp.where(counted, count.astype(f32), rows).astype(bf16)
    square_ref[...] = squares
    if not last:
        for copy in ahead:
            copy.wait()


def attend(inputs, side, sides, shift, following, before):
    queries, new_kv, kv_pool, page_table, ctx_len, residual_in, norm_gain = inputs
    slots, width = queries.shape
    pages, page, _ = kv_pool.shape
    tokens = pages * page
    step, columns = width // sides, new_kv.shape[1] // 2 // sides
    first, last = before is None, following is None
    vmem, anywhere = pl.BlockSpec(memory_space=pltpu.VMEM), pl.BlockSpec(memory_space=pl.ANY)
    smem = pl.BlockSpec(memory_space=pltpu.SMEM)
    kept = pltpu.VMEM((pages, page, columns), bf16)
    sems = pltpu.SemaphoreType.DMA((2, POOL_CUTS))
    out_shape = [
        jax.ShapeDtypeStruct((PAD, step), bf16),
        jax.ShapeDtypeStruct((slots, step), f32),
        jax.ShapeDtypeStruct((slots, HEAD), f32),
    ]
    scratch = []
    if first:
        gain = norm_gain.reshape(width // HEAD, HEAD)
        operands = [page_table, queries, new_kv, residual_in, gain, kv_pool]
        in_specs = [vmem] + [anywhere] * 5
        out_shape += [
            pltpu.VMEM(queries.shape, bf16),
            pltpu.VMEM(new_kv.shape, bf16),
            pltpu.VMEM(residual_in.shape, bf16),
            pltpu.VMEM(gain.shape, f32),
            pltpu.VMEM((PAD, tokens), f32),
        ]
        scratch += [kept, kept, pltpu.VMEM(gain.shape, bf16), sems, pltpu.SemaphoreType.DMA((4,))]
    else:
        operands = list(before)
        in_specs = [vmem] * 7
        if not last:
            operands.append(kv_pool)
            in_specs.append(anywhere)
    if not last:
        out_shape += [kept, kept]
        scratch.append(sems)
    send, mixed, squares, *rest = pl.pallas_call(
        functools.partial(attend_kernel, sides=sides, shift=shift, following=following, first=first),
        in_specs=[smem, smem] + in_specs,
        out_specs=[vmem] * len(out_shape),
        out_shape=out_shape,
        scratch_shapes=scratch,
        compiler_params=params(28),
        cost_estimate=cost(2e9, kv_pool.size),
        name="attend",
    )(ctx_len, side, *operands)
    if last:
        return send, mixed, squares, None
    return send, mixed, squares, rest if first else list(before[:5]) + rest


UP_TILE = 256
DOWN_TILE = 512


def tile_copy(w_ref, row, rows, column, buffer, sems, t, tile):
    at = pl.ds(pl.multiple_of(t * tile, tile), tile)
    source = w_ref.at[pl.ds(row, rows), pl.ds(pl.multiple_of(column + t * tile, tile), tile)]
    return pltpu.make_async_copy(source, buffer.at[:, at], sems.at[t])


def up_kernel(side, layout, *refs, parts, masks):
    refs = list(refs)
    gathered = [refs.pop(0) for _ in range(parts)]
    x_ref = None if parts else refs.pop(0)
    w_ref = refs.pop(0)
    if parts:
        x_ref = refs.pop(0)
    outs, (buffer, sems) = refs[:-2], refs[-2:]
    depth, width = buffer.shape[1:]
    tiles = width // UP_TILE

    def copy_of(n, t):
        column = pl.multiple_of((side[0] ^ masks[n]) * width, width)
        return tile_copy(w_ref, 0, depth, column, buffer.at[n], sems.at[n], t, UP_TILE)

    for n in range(len(masks)):
        for t in range(tiles):
            copy_of(n, t).start()
    if parts:
        rows, per = x_ref.shape[0], gathered[0].shape[0]
        pieces = per // PAD
        lane = lax.broadcasted_iota(i32, (rows, per), 1)
        row = lax.broadcasted_iota(i32, (rows, per), 0)
        picks = []
        for part in range(parts):
            target = jnp.full((rows, per), -1, i32)
            for piece in range(pieces):
                base = layout[part * pieces + piece]
                count = layout[(parts + part) * pieces + piece]
                inside = lane - piece * PAD
                mine = jnp.logical_and(inside >= 0, inside < count)
                target = jnp.where(mine, base + inside, target)
            picks.append((target == row).astype(f32).astype(bf16))

        @pl.loop(0, depth // UP_TILE)
        def _(t):
            at = pl.ds(pl.multiple_of(t * UP_TILE, UP_TILE), UP_TILE)
            total = jnp.zeros((rows, UP_TILE), f32)
            for part in range(parts):
                total = total + jnp.dot(
                    picks[part], gathered[part][:, at], preferred_element_type=f32
                )
            x_ref[:, at] = total.astype(bf16)

    for n, out_ref in enumerate(outs):

        @pl.loop(0, tiles)
        def _(t):
            copy_of(n, t).wait()
            at = pl.ds(pl.multiple_of(t * UP_TILE, UP_TILE), UP_TILE)
            out_ref[:, at] = jnp.dot(
                x_ref[...], buffer[n, :, at], preferred_element_type=f32
            ).astype(out_ref.dtype)


def up(side, layout, inputs, w_up, rows, width, dtype, masks, pack=False):
    depth = w_up.shape[0]
    vmem, smem = pl.BlockSpec(memory_space=pltpu.VMEM), pl.BlockSpec(memory_space=pltpu.SMEM)
    out = [jax.ShapeDtypeStruct((rows, width), dtype)] * len(masks)
    if pack:
        out = [jax.ShapeDtypeStruct((rows, depth), bf16)] + out
    return pl.pallas_call(
        functools.partial(up_kernel, parts=len(inputs) if pack else 0, masks=masks),
        in_specs=[smem, smem] + [vmem] * len(inputs) + [pl.BlockSpec(memory_space=pl.ANY)],
        out_specs=[vmem] * len(out),
        out_shape=out,
        scratch_shapes=[
            pltpu.VMEM((len(masks), depth, width), bf16),
            pltpu.SemaphoreType.DMA((len(masks), width // UP_TILE)),
        ],
        compiler_params=params(24),
        cost_estimate=cost(2 * rows * depth * width, depth * width * 2 * len(masks)),
        name="up",
    )(side, layout, *inputs, w_up)


def down_kernel(side, *refs, first, mask, ahead):
    refs = list(refs)
    a_ref, w_ref = refs.pop(0), refs.pop(0)
    before_ref = None if first else refs.pop(0)
    out_ref = refs.pop(0)
    next_ref = refs.pop(0) if ahead is not None else None
    buffer, sems = refs.pop(0), refs.pop(0)
    depth, width = buffer.shape
    tiles = width // DOWN_TILE

    def copy_of(other, buffer, sems, t):
        row = pl.multiple_of((side[0] ^ other) * depth, depth)
        return tile_copy(w_ref, row, depth, 0, buffer, sems, t, DOWN_TILE)

    for t in range(tiles):
        copy_of(mask, buffer, sems, t).start()
    if ahead is not None:
        for t in range(tiles):
            copy_of(ahead, next_ref, refs[0], t).start()

    @pl.loop(0, tiles)
    def _(t):
        copy_of(mask, buffer, sems, t).wait()
        at = pl.ds(pl.multiple_of(t * DOWN_TILE, DOWN_TILE), DOWN_TILE)
        part = jnp.dot(a_ref[...], buffer[:, at], preferred_element_type=f32)
        out_ref[:, at] = part if first else before_ref[:, at] + part

    if ahead is not None:

        @pl.loop(0, tiles)
        def _(t):
            copy_of(ahead, next_ref, refs[0], t).wait()


def down(side, active, w_down, before, mask, ahead=None):
    rows, depth = active.shape
    width = w_down.shape[1]
    vmem, smem = pl.BlockSpec(memory_space=pltpu.VMEM), pl.BlockSpec(memory_space=pltpu.SMEM)
    out = jax.ShapeDtypeStruct((rows, width), f32)
    sems = pltpu.SemaphoreType.DMA((width // DOWN_TILE,))
    return pl.pallas_call(
        functools.partial(down_kernel, first=before is None, mask=mask, ahead=ahead),
        in_specs=[smem, vmem, pl.BlockSpec(memory_space=pl.ANY)]
        + ([] if before is None else [vmem]),
        out_specs=vmem if ahead is None else [vmem, vmem],
        out_shape=out if ahead is None else [out, pltpu.VMEM((depth, width), bf16)],
        scratch_shapes=[pltpu.VMEM((depth, width), bf16), sems]
        + ([] if ahead is None else [sems]),
        compiler_params=params(24),
        cost_estimate=cost(2 * rows * depth * width, depth * width * 2),
        name="down",
    )(side, active, w_down, *([] if before is None else [before]))


def down_unpack_kernel(layout, a_ref, w_ref, before_ref, *refs, parts):
    outs, wide = refs[:-1], refs[-1]
    rows = a_ref.shape[0]
    width = w_ref.shape[1]
    tiles = width // DOWN_TILE
    tall = wide.shape[2] * tiles
    pieces = tall // (tiles * LIVE_CAP)
    row = lax.broadcasted_iota(i32, (PAD, rows), 0)
    column = lax.broadcasted_iota(i32, (PAD, rows), 1)
    picks = []
    for part in range(parts):
        some = []
        for piece in range(pieces):
            base = layout[part * pieces + piece]
            count = layout[(parts + part) * pieces + piece]
            some.append(jnp.logical_and(column - row == base, row < count).astype(f32))
        picks.append(jnp.concatenate(some, axis=0).astype(bf16))

    @pl.loop(0, tiles)
    def _(t):
        at = pl.ds(pl.multiple_of(t * DOWN_TILE, DOWN_TILE), DOWN_TILE)
        share = before_ref[:, at] + jnp.dot(a_ref[...], w_ref[:, at], preferred_element_type=f32)
        share = share.astype(bf16)
        for part in range(parts):
            back = jnp.dot(picks[part], share, preferred_element_type=f32)
            for piece in range(pieces):
                here = slice(piece * LIVE_CAP, (piece + 1) * LIVE_CAP)
                wide[t, part, here, :] = back[piece * PAD : piece * PAD + LIVE_CAP]

    across = parts // len(outs)
    for n, out in enumerate(outs):
        for k in range(across):
            part = PART_ORDER[n * across + k]
            for piece in range(pieces):
                here = slice(piece * LIVE_CAP, (piece + 1) * LIVE_CAP)
                whole = jnp.concatenate([wide[t, part, here, :] for t in range(tiles)], axis=0)
                start = k * tall + piece * tiles * LIVE_CAP
                out[start : start + tiles * LIVE_CAP, :] = whole.astype(bf16)


PART_ORDER = (0, 2, 1, 3)


def down_unpack(layout, active, weights, before, parts, pieces):
    rows, depth = active.shape
    width = weights.shape[1]
    tiles = width // DOWN_TILE
    tall = pieces * LIVE_CAP
    vmem, smem = pl.BlockSpec(memory_space=pltpu.VMEM), pl.BlockSpec(memory_space=pltpu.SMEM)
    return pl.pallas_call(
        functools.partial(down_unpack_kernel, parts=parts),
        in_specs=[smem, vmem, vmem, vmem],
        out_specs=[vmem] * 2,
        out_shape=[jax.ShapeDtypeStruct((parts // 2 * tall * tiles, DOWN_TILE), bf16)] * 2,
        scratch_shapes=[pltpu.VMEM((tiles, parts, tall, DOWN_TILE), f32)],
        compiler_params=params(24),
        cost_estimate=cost(2 * rows * depth * width, rows * width * 4),
        name="down_unpack",
    )(layout, active, weights, before)


def finish_kernel(lengths, side, *refs):
    out_ref = refs[-1]
    sides = (len(refs) - 1) // 3
    mixed, squares, blocks = refs[:sides], refs[sides : 2 * sides], refs[2 * sides : 3 * sides]
    slots, width = out_ref.shape
    step = width // sides
    total = squares[0][...]
    for other in squares[1:]:
        total = total + other[...]
    root = lax.rsqrt(jnp.sum(total, axis=-1, keepdims=True) / width + epsilon)
    gain = root * root
    tiles = step // DOWN_TILE
    picks = [
        live_pick(lengths, slots, tiles * LIVE_CAP, t * LIVE_CAP, True)[0] for t in range(tiles)
    ]
    for shift in range(sides):
        base = lax.rem(side[0] + shift, sides) * step
        block = blocks[shift][...]
        for t in range(tiles):
            back = jnp.dot(picks[t], block, preferred_element_type=f32)[:slots]
            at = pl.multiple_of(base + t * DOWN_TILE, DOWN_TILE)
            here = mixed[shift][:, t * DOWN_TILE : (t + 1) * DOWN_TILE]
            out_ref[:, pl.ds(at, DOWN_TILE)] = (here + gain * back).astype(bf16)


def finish(ctx_len, side, mixed, squares, blocks):
    vmem, smem = pl.BlockSpec(memory_space=pltpu.VMEM), pl.BlockSpec(memory_space=pltpu.SMEM)
    slots, width = mixed[0].shape[0], mixed[0].shape[1] * len(mixed)
    return pl.pallas_call(
        finish_kernel,
        in_specs=[smem, smem] + [vmem] * (3 * len(mixed)),
        out_specs=vmem,
        out_shape=jax.ShapeDtypeStruct((slots, width), bf16),
        compiler_params=params(16),
        cost_estimate=cost(slots * width * 32, slots * width * 8),
        name="finish",
    )(ctx_len, side, *mixed, *squares, *blocks)


def swap(x, axis, count, mask):
    return lax.ppermute(x, axis, [(j, j ^ mask) for j in range(count)])


def shifted(x, axis, count, shift):
    return lax.ppermute(x, axis, [(j, (j + shift) % count) for j in range(count)])


def added(a, b):
    return (a.astype(f32) + b.astype(f32)).astype(bf16)


def tie(x, *others):
    return lax.optimization_barrier((x, *others))[0]


def feed_forward(rows, side, layout, gathered, w_up, w_down):
    width = w_up.shape[1] // 4
    packed, far_partner = up(side, layout, gathered, w_up, rows, width, bf16, (3,), pack=True)
    met = swap(far_partner, "side", 4, 1)
    far, near = up(side, layout, [packed], w_up, rows, width, bf16, (2, 1))
    met = tie(met, far)
    pair_sum = added(far, met)
    crossed = swap(pair_sum, "side", 4, 2)
    near = swap(tie(near, met), "side", 4, 1)
    (own,) = up(side, layout, [tie(packed, pair_sum)], w_up, rows, width, f32, (0,))
    lifted = own + near.astype(f32) + crossed.astype(f32)
    clipped = jnp.maximum(lifted, 0.0)
    active = (clipped * clipped).astype(bf16)
    across = swap(active, "side", 4, 2)
    beside = swap(active, "side", 4, 1)
    total = down(side, active, w_down, None, 0)
    total = down(side, beside, w_down, total, 1)
    across, total = lax.optimization_barrier((across, total))
    forwarded = swap(across, "side", 4, 1)
    total, weights = down(side, across, w_down, total, 2, ahead=3)
    parts, pieces = len(gathered), gathered[0].shape[0] // PAD
    return down_unpack(layout, forwarded, weights, total, parts, pieces)


def layout_kernel(side, shard, *refs, limits):
    parts, out, step_out = refs[:-2], refs[-2], refs[-1]
    pieces = parts[0].shape[0] // PAD
    devices = len(parts) * pieces
    counts, places = [], []
    for part in range(len(parts)):
        for piece in range(pieces):
            last = parts[part][piece * PAD : (piece + 1) * PAD, :].astype(f32)[PAD - 1 :]
            counts.append(jnp.max(last).astype(i32))
            places.append(lax.rem(side[0] - piece + pieces, pieces) * len(parts) + (shard[0] ^ part))
    total = jnp.int32(0)
    for one in range(devices):
        base = jnp.int32(0)
        for other in range(devices):
            base = base + jnp.where(places[other] < places[one], counts[other], 0)
        out[one] = base
        out[devices + one] = counts[one]
        total = total + counts[one]
    step = jnp.int32(0)
    for limit in limits:
        step = step + (total > limit).astype(i32)
    step_out[0] = step


def read_layout(side, shard, gathered, limits):
    per = gathered[0].shape[0]
    pieces = per // PAD
    scalars = pl.BlockSpec(memory_space=pltpu.SMEM)
    return pl.pallas_call(
        functools.partial(layout_kernel, limits=limits),
        grid=(1,),
        in_specs=[scalars, scalars] + [pl.BlockSpec((per, 128), lambda t: (0, 0))] * len(gathered),
        out_specs=[scalars, scalars],
        out_shape=[
            jax.ShapeDtypeStruct((2 * len(gathered) * pieces,), i32),
            jax.ShapeDtypeStruct((1,), i32),
        ],
        compiler_params=params(16),
        name="layout",
    )(side, shard, *gathered)


ROW_STEPS = (112, 128, 144, 160, 192)


def line_shards(
    queries, new_kv, kv_pool, page_table, ctx_len, residual_in, norm_gain, w_up, w_down
):
    i, s = lax.axis_index("side"), lax.axis_index("shard")
    side, shard = i.reshape(1), s.reshape(1)
    in_hbm = lambda x: pltpu.with_memory_space_constraint(x, pltpu.HBM)
    queries, new_kv, kv_pool, page_table, ctx_len, residual_in, w_up, w_down = map(
        in_hbm, (queries, new_kv, kv_pool, page_table, ctx_len, residual_in, w_up, w_down)
    )
    inputs = queries, new_kv, kv_pool, page_table, ctx_len, residual_in, norm_gain
    mixed, squares, arrived, kept = [None] * 4, [None] * 4, [None] * 4, None
    for shift, following in zip(SHIFTS, SHIFTS[1:] + (None,)):
        send, mixed[shift], squares[shift], kept = attend(inputs, side, 4, shift, following, kept)
        arrived[shift] = shifted(send, "side", 4, shift) if shift else send
    here = jnp.concatenate(arrived, axis=0)
    by_x = swap(here, "shard", 4, 2)
    by_core = swap(here, "shard", 4, 1)
    by_both = swap(by_x, "shard", 4, 1)
    gathered = [here, by_core, by_x, by_both]
    layout, step = read_layout(side, shard, gathered, ROW_STEPS[:-1])
    stay, leave = lax.switch(
        step[0],
        [functools.partial(feed_forward, rows) for rows in ROW_STEPS],
        side, layout, gathered, w_up, w_down,
    )
    back = swap(leave, "shard", 4, 1)
    half = back.shape[0] // 2
    to_x = added(stay[half:], back[half:])
    kept = added(stay[:half], back[:half])
    home = added(kept, swap(to_x, "shard", 4, 2)).reshape(4, half // 4, -1)
    blocks = [home[0]] + [shifted(home[shift], "side", 4, -shift) for shift in (1, 2, 3)]
    return finish(ctx_len, side, mixed, squares, blocks)


def attend_slots(queries, new_kv, pool_pages, page_rows, lengths):
    slot_count = queries.shape[0]
    positions = page_rows.shape[1] * pool_pages.shape[1]
    fetched = pool_pages[page_rows].reshape(slot_count, positions, 2, KV_HEADS, HEAD)
    fresh_kv = new_kv.reshape(slot_count, 2, KV_HEADS, HEAD)
    query_heads = queries.reshape(slot_count, KV_HEADS, GROUP, HEAD)
    score_scale = 1.0 / math.sqrt(HEAD)
    scores = (
        jnp.einsum("sgqd,slgd->sgql", query_heads, fetched[:, :, 0], preferred_element_type=f32)
        * score_scale
    )
    own_score = (
        jnp.einsum("sgqd,sgd->sgq", query_heads, fresh_kv[:, 0], preferred_element_type=f32)
        * score_scale
    )
    visible = (jnp.arange(positions, dtype=i32)[None, :] < lengths[:, None])[:, None, None, :]
    scores = jnp.where(visible, scores, -1e30)
    highest = jnp.maximum(jnp.max(scores, axis=-1), own_score)
    weights = jnp.where(visible, jnp.exp(scores - highest[..., None]), 0.0)
    own_weight = jnp.exp(own_score - highest)
    denominator = jnp.sum(weights, axis=-1) + own_weight
    probabilities = (weights / denominator[..., None]).astype(bf16)
    own_prob = (own_weight / denominator).astype(bf16).astype(f32)
    attended = jnp.einsum(
        "sgql,slgd->sgqd", probabilities, fetched[:, :, 1], preferred_element_type=f32
    )
    attended = attended + own_prob[..., None] * fresh_kv[:, 1].astype(f32)[:, :, None, :]
    return attended.reshape(slot_count, -1)


def any_shards(queries, new_kv, kv_pool, page_table, ctx_len, residual_in, norm_gain, w_up, w_down):
    attended = attend_slots(queries, new_kv, kv_pool, page_table, ctx_len)
    mixed_rows = residual_in.astype(f32) + attended
    mean_square = jnp.mean(mixed_rows * mixed_rows, axis=-1, keepdims=True)
    normed = (mixed_rows * lax.rsqrt(mean_square + epsilon) * norm_gain.astype(f32)).astype(bf16)
    live_mask = ctx_len > 0
    spread = lax.all_to_all(normed, "side", split_axis=1, concat_axis=0, tiled=True)
    up_partial = jnp.dot(
        lax.all_gather(spread, "shard", axis=0, tiled=True), w_up, preferred_element_type=f32
    )
    lifted = lax.psum(up_partial, "side")
    clipped = jnp.maximum(lifted, 0.0)
    active = (clipped * clipped).astype(bf16)
    down_share = lax.psum_scatter(
        jnp.dot(active, w_down, preferred_element_type=f32).astype(bf16),
        "shard",
        scatter_dimension=0,
        tiled=True,
    )
    returned = lax.all_to_all(down_share, "side", split_axis=0, concat_axis=1, tiled=True)
    returned = jnp.where(live_mask[:, None], returned.astype(f32), 0.0)
    return (mixed_rows + returned).astype(bf16)


def solution(mesh):
    rows = ("grp", "side", "shard")
    placed = (
        P(rows, None),
        P(rows, None),
        P(rows, None, None),
        P(rows, None),
        P(rows),
        P(rows, None),
        P(),
        P("side", "shard"),
        P("shard", "side"),
    )
    square = mesh.shape["side"] == 4 and mesh.shape["shard"] == 4
    return jax.shard_map(
        line_shards if square else any_shards,
        mesh=mesh,
        in_specs=placed,
        out_specs=P(rows, None),
        check_vma=False,
    )
```

time: 270 us -> 107 us (0.40)
  waiting for transfers between devices: 154 us -> 41.6 us
  Pallas kernels: 0 us -> 40.1 us
  blocking collectives: 39.4 us -> 0 us
  local copies, waits for them, and re-layouts: 28.2 us -> 0.76 us
  matrix products: 24.8 us -> 0 us
  starting transfers between devices: 4.7 us -> 23.2 us
  between operations: 14.4 us -> 0.75 us
  other arithmetic: 3.09 us -> 0.34 us
    psum x1 -> x0, waiting for transfers between devices: 145 us -> none  [shards(): lifted = lax.psum(up_partial, 'side')]
    ppermute x0 -> x17, waiting for transfers between devices: none -> 41.6 us  [the longest x11 35.9 us: swap(): return lax.ppermute(x, axis, [(j, j ^ mask) for j in range(count)])]
    pallas_call x0 -> x13, Pallas kernels: none -> 40.1 us  [the longest x4 14 us: attend(): pl.pallas_call(functools.partial(attend_kernel, sides=sides, shift=shift,...]
    dot_general x5 -> x0, matrix products: 24.8 us -> none  [the longest x1 11.2 us: shards(): jnp.dot(active, w_down, preferred_element_type=jnp.float32)]
    ppermute x0 -> x17, starting transfers between devices: none -> 23.2 us  [the longest x11 12.3 us: swap(): return lax.ppermute(x, axis, [(j, j ^ mask) for j in range(count)])]
    all_to_all x1 -> x0, blocking collectives: 15.2 us -> none  [shards(): lax.all_to_all(normed, 'side', split_axis=1, concat_axis=0, tiled=True)]
    unnamed x1 -> x0, blocking collectives: 14.4 us -> none
    gather x1 -> x0, local copies, waits for them, and re-layouts: 12.4 us -> none  [attend_slots(): pool_pages[page_rows].reshape(slot_count, positions, 2, KV_HEADS, HEAD)]
  transfers between devices with their start and end apart: 3 -> 17, of which waited for: 2 -> 13; matrix products, arithmetic and copies ran while one was open for 0% -> 0% of each run, Pallas kernels for 0% -> 21%
where the time goes in v3:
time: 107 us
  waiting for transfers between devices  41.6 us (39%)
  Pallas kernels  40.1 us (37%)
  starting transfers between devices  23.2 us (22%)
    ppermute x11, waiting for transfers between devices, swap(): return lax.ppermute(x, axis, [(j, j ^ mask) for j in range(count)])  35.9 us
    pallas_call x4, Pallas kernels, attend(): pl.pallas_call(functools.partial(attend_kernel, sides=sides, shift=shift,...  14 us
    ppermute x11, starting transfers between devices, swap(): return lax.ppermute(x, axis, [(j, j ^ mask) for j in range(count)])  12.3 us
    pallas_call x3, Pallas kernels, up(): pl.pallas_call(functools.partial(up_kernel, parts=len(inputs) if pack els...  11.7 us
    ppermute x6, starting transfers between devices, shifted(): lax.ppermute(x, axis, [(j, (j + shift) % count) for j in range(count)])  10.9 us
    pallas_call x3, Pallas kernels, down(): pl.pallas_call(functools.partial(down_kernel, first=before is None, mask=...  8.79 us
    ppermute x6, waiting for transfers between devices, shifted(): lax.ppermute(x, axis, [(j, (j + shift) % count) for j in range(count)])  5.69 us
    pallas_call x1, Pallas kernels, down_unpack(): pl.pallas_call(functools.partial(down_unpack_kernel, parts=parts), in_spe...  2.89 us
  transfers between devices with their start and end apart: 17, of which 13 were waited for; matrix products, arithmetic and copies ran while one was open for 0% of the time, Pallas kernels for 21%

profile of v3, /device:TPU:0, one launch (start us, length us, event | category | flops | bytes accessed | tf_op | source)
XLA Modules:
  0.0 107.2 jit_solution(16398456045371901321)
XLA Ops:
  0.0 0.7 copy-done
  0.7 4.3 %attend.4 = (bf16[16,2048]{1,0:T(8,128)(2,1)S(1)}, f32[15,2048]{1,0:T(8,128)S(1)}, f32[15,128]{1,0:T(8,128)S(1)}, bf16[15,8192]{1,0:T(8,128)(2,1)S(1)}, bf16[15,...) custom-call(s32[15]{0:T(128)} %lengths.9, ...), custom_call_target="tpu_custom_call" | custom-call | flops 2000000000 | bytes 3670016 | tf_op jit(solution)/shard_map/attend/pallas_call | solution.py:236
  5.0 3.7 %attend.5 = (bf16[16,2048]{1,0:T(8,128)(2,1)S(1)}, f32[15,2048]{1,0:T(8,128)S(1)}, f32[15,128]{1,0:T(8,128)S(1)}, bf16[112,16,256]{2,1,0:T(8,128)(2,1)S(1)}, bf16[112,16,256]{2,1,0:T(8,128)(2,1)S(1)}) custom-call(s32[15]{0:T(128)} %lengths.9, s32[1]{0:T(128)} %bitcast.side, bf16[15,8192]{1,0:T(8,128)(2,1)S(1)} %get-tuple-element.207.refs_0_, ...), custom_call_target="tpu_custom_call" | custom-call | flops 2000000000 | bytes 3670016 | tf_op jit(solution)/shard_map/attend/pallas_call | solution.py:236
  8.8 3.1 %collective-permute-start.30 = (bf16[16,2048]{1,0:T(8,128)(2,1)S(1)}, bf16[16,2048]{1,0:T(8,128)(2,1)S(1)}, u32[]{:S(2)}, u32[]{:S(2)}) collective-permute-start(bf16[16,2048]{1,0:T(8,128)(2,1)S(1)} %get-tuple-element.227), channel_id=1, source_target_pairs={{0,4},{4,8},{8,12},{12,0},{1,5},{5,9},{9,13},{13,1},{2,6},{6,10},{... | collective-permute-start | bytes 196616 | tf_op jit(solution)/shard_map/ppermute | solution.py:496
  11.8 2.6 %collective-permute-start.31 = (bf16[16,2048]{1,0:T(8,128)(2,1)S(1)}, bf16[16,2048]{1,0:T(8,128)(2,1)S(1)}, u32[]{:S(2)}, u32[]{:S(2)}) collective-permute-start(bf16[16,2048]{1,0:T(8,128)(2,1)S(1)} %get-tuple-element.228), channel_id=1, source_target_pairs={{0,8},{4,12},{8,0},{12,4},{1,9},{5,13},{9,1},{13,5},{2,10},{6,14},... | collective-permute-start | bytes 196616 | tf_op jit(solution)/shard_map/ppermute | solution.py:496
  14.4 3.7 %attend.6 = (bf16[16,2048]{1,0:T(8,128)(2,1)S(1)}, f32[15,2048]{1,0:T(8,128)S(1)}, f32[15,128]{1,0:T(8,128)S(1)}, bf16[112,16,256]{2,1,0:T(8,128)(2,1)S(1)}, bf16[112,16,256]{2,1,0:T(8,128)(2,1)S(1)}) custom-call(s32[15]{0:T(128)} %lengths.9, s32[1]{0:T(128)} %bitcast.side, bf16[15,8192]{1,0:T(8,128)(2,1)S(1)} %get-tuple-element.207.refs_0_, ...), custom_call_target="tpu_custom_call" | custom-call | flops 2000000000 | bytes 3670016 | tf_op jit(solution)/shard_map/attend/pallas_call | solution.py:236
  18.2 1.4 %collective-permute-start.32 = (bf16[16,2048]{1,0:T(8,128)(2,1)S(1)}, bf16[16,2048]{1,0:T(8,128)(2,1)S(1)}, u32[]{:S(2)}, u32[]{:S(2)}) collective-permute-start(bf16[16,2048]{1,0:T(8,128)(2,1)S(1)} %get-tuple-element.229), channel_id=1, source_target_pairs={{0,12},{4,0},{8,4},{12,8},{1,13},{5,1},{9,5},{13,9},{2,14},{6,2},{... | collective-permute-start | bytes 196616 | tf_op jit(solution)/shard_map/ppermute | solution.py:496
  19.6 2.2 %attend.7 = (bf16[16,2048]{1,0:T(8,128)(2,1)S(1)}, f32[15,2048]{1,0:T(8,128)S(1)}, f32[15,128]{1,0:T(8,128)S(1)}) custom-call(s32[15]{0:T(128)} %lengths.9, s32[1]{0:T(128)} %bitcast.side, bf16[15,8192]{1,0:T(8,128)(2,1)S(1)} %get-tuple-element.207.refs_0_, bf16[15,2048]{1,0:T(8,128)(2,1)S(1)} %get-tuple-element.208.refs_1_, ...), custom_call_target="tpu_custom_call" | custom-call | flops 2000000000 | bytes 3670016 | tf_op jit(solution)/shard_map/attend/pallas_call | solution.py:236
  21.8 0.0 collective-permute-done.31
  21.8 0.6 collective-permute-done.32
  22.5 1.5 %collective-permute-start.34 = (bf16[64,2048]{1,0:T(8,128)(2,1)S(1)}, bf16[64,2048]{1,0:T(8,128)(2,1)S(1)}, u32[]{:S(2)}, u32[]{:S(2)}) collective-permute-start(bf16[64,2048]{1,0:T(8,128)(2,1)S(1)} %constant_dynamic-update-slice_fusion.refs_0_), channel_id=1, source_target_pairs={{0,2},{1,3},{2,0},{3,1},{4,6},{5,7},{6,4},{7,5},{8,10},{9,11},{10,... | collective-permute-start | bytes 786440 | tf_op jit(solution)/shard_map/ppermute | solution.py:492
  24.0 0.0 collective-permute-start.33
  24.0 5.2 %collective-permute-done.34.refs_2_ = bf16[64,2048]{1,0:T(8,128)(2,1)S(1)} collective-permute-done((bf16[64,2048]{1,0:T(8,128)(2,1)S(1)}, bf16[64,2048]{1,0:T(8,128)(2,1)S(1)}, u32[]{:S(2)}, u32[]{:S(2)}) %collective-permute-start.34) | collective-permute-done | bytes 262176 | tf_op jit(solution)/shard_map/ppermute | solution.py:492
  29.1 1.5 %collective-permute-done.35.refs_3_ = bf16[64,2048]{1,0:T(8,128)(2,1)S(1)} collective-permute-done((bf16[64,2048]{1,0:T(8,128)(2,1)S(1)}, bf16[64,2048]{1,0:T(8,128)(2,1)S(1)}, u32[]{:S(2)}, u32[]{:S(2)}) %collective-permute-start.35) | collective-permute-done | bytes 262176 | tf_op jit(solution)/shard_map/ppermute | solution.py:492
  30.7 1.2 %layout.1 = (s32[32]{0:T(128)S(1)}, s32[1]{0:T(128)}) custom-call(s32[1]{0:T(128)} %bitcast.side, s32[1]{0:T(128)} %bitcast.2.shard, bf16[64,2048]{1,0:T(8,128)(2,1)S(1)} %constant_dynamic-update-slice_fusion.refs_0_, bf16[64,2048]{1,0:T(8,128)(2,1)S(1)} %collective-permute-done.33.refs_1_, bf16[64,2048]{1,0:T(8,128)(2,1)S(1)} %collective-permute-done.34.refs_2_, ...), custom_call_target="tpu_custom_call" | custom-call | tf_op jit(solution)/shard_map/layout/pallas_call | solution.py:559
  32.5 55.3 %conditional.1 = ((bf16[384,512]{1,0:T(8,128)(2,1)S(1)}, bf16[384,512]{1,0:T(8,128)(2,1)S(1)})) conditional(s32[]{:T(128)} %bitcast.3, (s32[1]{0:T(128)}, s32[32]{0:T(128)S(1)}, bf16[64,2048]{1,0:T(8,128)(2,1)S(1)}, bf16[64,2048]{1,0:T(8,128)(2,1)S(1)}, bf16[64,2048]{1,0:T(8,128)(2,1)S(1)}, ...), branch_computations={%region_0.0_spmd, %region_1.0_spmd, %region_2.0_spmd, %region_3.0_... | conditional | flops 5639307264 | bytes 43516152 | solution.py:596
  32.7 3.8 %up.21 = (bf16[144,2048]{1,0:T(8,128)(2,1)S(1)}, bf16[144,1024]{1,0:T(8,128)(2,1)S(1)}) custom-call(s32[1]{0:T(128)} %get-tuple-element.124.side, s32[32]{0:T(128)S(1)} %get-tuple-element.123.layout, bf16[64,2048]{1,0:T(8,128)(2,1)S(1)} %get-tuple-element.125.refs_0_, bf16[64,2048]{1,0:T(8,128)(2,1)S(1)} %get-tuple-element.126.refs_1_, ...), custom_call_target="tpu_custom_call" | custom-call | flops 603979776 | bytes 4194304 | tf_op jit(solution)/shard_map/cond/branch_2_fun/up/pallas_call | solution.py:322
  36.5 0.7 collective-permute-start.12
  37.2 4.7 %up.22 = (bf16[144,1024]{1,0:T(8,128)(2,1)S(1)}, bf16[144,1024]{1,0:T(8,128)(2,1)S(1)}) custom-call(s32[1]{0:T(128)} %get-tuple-element.124.side, s32[32]{0:T(128)S(1)} %get-tuple-element.123.layout, bf16[144,2048]{1,0:T(8,128)(2,1)S(1)} %get-tuple-element.134.refs_0_, bf16[2048,4096]{1,0:T(8,128)(2,1)} %get-tuple-element.129.refs_4_.refs_1_), custom_call_target="tpu_custom_call" | custom-call | flops 603979776 | bytes 8388608 | tf_op jit(solution)/shard_map/cond/branch_2_fun/up/pallas_call | solution.py:322
  41.9 3.7 %collective-permute-done.12 = bf16[144,1024]{1,0:T(8,128)(2,1)S(1)} collective-permute-done((bf16[144,1024]{1,0:T(8,128)(2,1)S(1)}, bf16[144,1024]{1,0:T(8,128)(2,1)S(1)}, u32[]{:S(2)}, u32[]{:S(2)}) %collective-permute-start.12) | collective-permute-done | bytes 294944 | tf_op jit(solution)/shard_map/cond/branch_2_fun/ppermute | solution.py:492
  45.6 0.1 add_convert_fusion.2
  45.7 0.7 collective-permute-start.13
  46.4 2.8 %collective-permute-start.14 = (bf16[144,1024]{1,0:T(8,128)(2,1)S(1)}, bf16[144,1024]{1,0:T(8,128)(2,1)S(1)}, u32[]{:S(2)}, u32[]{:S(2)}) collective-permute-start(bf16[144,1024]{1,0:T(8,128)(2,1)S(1)} %add_convert_fusion.2), channel_id=1, source_target_pairs={{0,8},{4,12},{8,0},{12,4},{1,9},{5,13},{9,1},{13,5},{2,10},{6,14},... | collective-permute-start | bytes 884744 | tf_op jit(solution)/shard_map/cond/branch_2_fun/ppermute | solution.py:492
  49.2 3.2 %up.23 = f32[144,1024]{1,0:T(8,128)S(1)} custom-call(s32[1]{0:T(128)} %get-tuple-element.124.side, s32[32]{0:T(128)S(1)} %get-tuple-element.123.layout, bf16[144,2048]{1,0:T(8,128)(2,1)S(1)} %get-tuple-element.134.refs_0_, bf16[2048,4096]{1,0:T(8,128)(2,1)} %get-tuple-element.129.refs_4_.refs_1_), custom_call_target="tpu_custom_call" | custom-call | flops 603979776 | bytes 4194304 | tf_op jit(solution)/shard_map/cond/branch_2_fun/up/pallas_call | solution.py:322
  52.4 7.9 %collective-permute-done.13 = bf16[144,1024]{1,0:T(8,128)(2,1)S(1)} collective-permute-done((bf16[144,1024]{1,0:T(8,128)(2,1)S(1)}, bf16[144,1024]{1,0:T(8,128)(2,1)S(1)}, u32[]{:S(2)}, u32[]{:S(2)}) %collective-permute-start.13) | collective-permute-done | bytes 294944 | tf_op jit(solution)/shard_map/cond/branch_2_fun/ppermute | solution.py:492
  60.3 0.0 collective-permute-done.14
  60.3 0.1 multiply_convert_fusion.2.refs_0_
  60.4 2.1 %collective-permute-start.16 = (bf16[144,1024]{1,0:T(8,128)(2,1)S(1)}, bf16[144,1024]{1,0:T(8,128)(2,1)S(1)}, u32[]{:S(2)}, u32[]{:S(2)}) collective-permute-start(bf16[144,1024]{1,0:T(8,128)(2,1)S(1)} %multiply_convert_fusion.2.refs_0_), channel_id=1, source_target_pairs={{0,4},{4,0},{8,12},{12,8},{1,5},{5,1},{9,13},{13,9},{2,6},{6,2},{1... | collective-permute-start | bytes 884744 | tf_op jit(solution)/shard_map/cond/branch_2_fun/ppermute | solution.py:492
  62.5 2.8 %collective-permute-start.15 = (bf16[144,1024]{1,0:T(8,128)(2,1)S(1)}, bf16[144,1024]{1,0:T(8,128)(2,1)S(1)}, u32[]{:S(2)}, u32[]{:S(2)}) collective-permute-start(bf16[144,1024]{1,0:T(8,128)(2,1)S(1)} %multiply_convert_fusion.2.refs_0_), channel_id=1, source_target_pairs={{0,8},{4,12},{8,0},{12,4},{1,9},{5,13},{9,1},{13,5},{2,10},{6,14},... | collective-permute-start | bytes 884744 | tf_op jit(solution)/shard_map/cond/branch_2_fun/ppermute | solution.py:492
  65.3 2.6 %down.21.refs_2_ = f32[144,2048]{1,0:T(8,128)S(1)} custom-call(s32[1]{0:T(128)} %get-tuple-element.124.side, bf16[144,1024]{1,0:T(8,128)(2,1)S(1)} %multiply_convert_fusion.2.refs_0_, bf16[4096,2048]{1,0:T(8,128)(2,1)} %get-tuple-element.137.refs_1_), custom_call_target="tpu_custom_call" | custom-call | flops 603979776 | bytes 4194304 | tf_op jit(solution)/shard_map/cond/branch_2_fun/down/pallas_call | solution.py:377
  67.9 4.9 %collective-permute-done.16.refs_0_ = bf16[144,1024]{1,0:T(8,128)(2,1)S(1)} collective-permute-done((bf16[144,1024]{1,0:T(8,128)(2,1)S(1)}, bf16[144,1024]{1,0:T(8,128)(2,1)S(1)}, u32[]{:S(2)}, u32[]{:S(2)}) %collective-permute-start.16) | collective-permute-done | bytes 294944 | tf_op jit(solution)/shard_map/cond/branch_2_fun/ppermute | solution.py:492
  72.9 2.6 %down.22.refs_2_ = f32[144,2048]{1,0:T(8,128)S(1)} custom-call(s32[1]{0:T(128)} %get-tuple-element.124.side, bf16[144,1024]{1,0:T(8,128)(2,1)S(1)} %collective-permute-done.16.refs_0_, bf16[4096,2048]{1,0:T(8,128)(2,1)} %get-tuple-element.137.refs_1_, f32[144,2048]{1,0:T(8,128)S(1)} %down.21.refs_2_), custom_call_target="tpu_custom_call" | custom-call | flops 603979776 | bytes 4194304 | tf_op jit(solution)/shard_map/cond/branch_2_fun/down/pallas_call | solution.py:377
  75.5 1.7 %collective-permute-done.15.refs_0_ = bf16[144,1024]{1,0:T(8,128)(2,1)S(1)} collective-permute-done((bf16[144,1024]{1,0:T(8,128)(2,1)S(1)}, bf16[144,1024]{1,0:T(8,128)(2,1)S(1)}, u32[]{:S(2)}, u32[]{:S(2)}) %collective-permute-start.15) | collective-permute-done | bytes 294944 | tf_op jit(solution)/shard_map/cond/branch_2_fun/ppermute | solution.py:492
  77.2 3.6 %down.23 = (f32[144,2048]{1,0:T(8,128)S(1)}, bf16[1024,2048]{1,0:T(8,128)(2,1)S(1)}) custom-call(s32[1]{0:T(128)} %get-tuple-element.124.side, bf16[144,1024]{1,0:T(8,128)(2,1)S(1)} %collective-permute-done.15.refs_0_, bf16[4096,2048]{1,0:T(8,128)(2,1)} %get-tuple-element.137.refs_1_, f32[144,2048]{1,0:T(8,128)S(1)} %down.22.refs_2_), custom_call_target="tpu_custom_call" | custom-call | flops 603979776 | bytes 4194304 | tf_op jit(solution)/shard_map/cond/branch_2_fun/down/pallas_call | solution.py:377
  80.7 3.9 %collective-permute-done.17.a_ref = bf16[144,1024]{1,0:T(8,128)(2,1)S(1)} collective-permute-done((bf16[144,1024]{1,0:T(8,128)(2,1)S(1)}, bf16[144,1024]{1,0:T(8,128)(2,1)S(1)}, u32[]{:S(2)}, u32[]{:S(2)}) %collective-permute-start.17) | collective-permute-done | bytes 294944 | tf_op jit(solution)/shard_map/cond/branch_2_fun/ppermute | solution.py:492
  84.6 2.9 %down_unpack.7 = (bf16[384,512]{1,0:T(8,128)(2,1)S(1)}, bf16[384,512]{1,0:T(8,128)(2,1)S(1)}) custom-call(s32[32]{0:T(128)S(1)} %get-tuple-element.123.layout, bf16[144,1024]{1,0:T(8,128)(2,1)S(1)} %collective-permute-done.17.a_ref, bf16[1024,2048]{1,0:T(8,128)(2,1)S(1)} %get-tuple-element.140.w_ref, f32[144,2048]{1,0:T(8,128)S(1)} %get-tuple-element.141.before_ref), custom_call_target="tpu_custom_call" | custom-call | flops 603979776 | bytes 1179648 | tf_op jit(solution)/shard_map/cond/branch_2_fun/down_unpack/pallas_call | solution.py:440
  87.8 0.1 collective-permute-start.36
  87.8 1.7 %collective-permute-done.36 = bf16[384,512]{1,0:T(8,128)(2,1)S(1)} collective-permute-done((bf16[384,512]{1,0:T(8,128)(2,1)S(1)}, bf16[384,512]{1,0:T(8,128)(2,1)S(1)}, u32[]{:S(2)}, u32[]{:S(2)}) %collective-permute-start.36) | collective-permute-done | bytes 393248 | tf_op jit(solution)/shard_map/ppermute | solution.py:492
  89.6 0.1 add_convert_fusion.6
  89.6 1.6 %collective-permute-start.37 = (bf16[192,512]{1,0:T(8,128)(2,1)S(1)}, bf16[192,512]{1,0:T(8,128)(2,1)S(1)}, u32[]{:S(2)}, u32[]{:S(2)}) collective-permute-start(bf16[192,512]{1,0:T(8,128)(2,1)S(1)} %add_convert_fusion.6), channel_id=1, source_target_pairs={{0,2},{1,3},{2,0},{3,1},{4,6},{5,7},{6,4},{7,5},{8,10},{9,11},{10,... | collective-permute-start | bytes 589832 | tf_op jit(solution)/shard_map/ppermute | solution.py:492
  91.2 5.4 %collective-permute-done.37 = bf16[192,512]{1,0:T(8,128)(2,1)S(1)} collective-permute-done((bf16[192,512]{1,0:T(8,128)(2,1)S(1)}, bf16[192,512]{1,0:T(8,128)(2,1)S(1)}, u32[]{:S(2)}, u32[]{:S(2)}) %collective-permute-start.37) | collective-permute-done | bytes 196640 | tf_op jit(solution)/shard_map/ppermute | solution.py:492
  96.6 0.1 add_convert_fusion.5
  96.7 3.0 %collective-permute-start.38 = (bf16[48,512]{1,0:T(8,128)(2,1)S(1)}, bf16[48,512]{1,0:T(8,128)(2,1)S(1)}, u32[]{:S(2)}, u32[]{:S(2)}) collective-permute-start(bf16[48,512]{1,0:T(8,128)(2,1)S(1)} %get-tuple-element.236), channel_id=1, source_target_pairs={{0,12},{4,0},{8,4},{12,8},{1,13},{5,1},{9,5},{13,9},{2,14},{6,2},{... | collective-permute-start | bytes 147464 | tf_op jit(solution)/shard_map/ppermute | solution.py:496
  99.7 0.8 collective-permute-start.40
  100.5 0.9 collective-permute-done.38.refs_9_
  101.4 3.2 %collective-permute-done.39.refs_10_ = bf16[48,512]{1,0:T(8,128)(2,1)S(1)} collective-permute-done((bf16[48,512]{1,0:T(8,128)(2,1)S(1)}, bf16[48,512]{1,0:T(8,128)(2,1)S(1)}, u32[]{:S(2)}, u32[]{:S(2)}) %collective-permute-start.39) | collective-permute-done | bytes 49184 | tf_op jit(solution)/shard_map/ppermute | solution.py:496
  104.7 0.9 collective-permute-done.40.refs_11_
  105.6 1.6 %finish.1 = bf16[15,8192]{1,0:T(8,128)(2,1)} custom-call(s32[15]{0:T(128)} %lengths.9, s32[1]{0:T(128)} %bitcast.side, f32[15,2048]{1,0:T(8,128)S(1)} %get-tuple-element.218.refs_0_, f32[15,2048]{1,0:T(8,128)S(1)} %get-tuple-element.219.refs_1_, f32[15,2048]{1,0:T(8,128)S(1)} %get-tuple-element.220.refs_2_, f32[15,2048]{1,0:T(8,128)S(1)} %get-tuple-element.221.refs_3_, ...), custom_call_target="tpu_custom_call" | custom-call | flops 3932160 | bytes 983040 | tf_op jit(solution)/shard_map/finish/pallas_call | solution.py:480
  (11 shorter events, 0.1 us)
Async XLA Ops:
  0.0 0.7 copy-start
  8.8 13.0 %collective-permute-start.30 = (bf16[16,2048]{1,0:T(8,128)(2,1)S(1)}, bf16[16,2048]{1,0:T(8,128)(2,1)S(1)}, u32[]{:S(2)}, u32[]{:S(2)}) collective-permute-start(bf16[16,2048]{1,0:T(8,128)(2,1)S(1)} %get-tuple-element.227), channel_id=1, source_target_pairs={{0,4},{4,8},{8,12},{12,0},{1,5},{5,9},{9,13},{13,1},{2,6},{6,10},{... | collective-permute-start | bytes 196616 | tf_op jit(solution)/shard_map/ppermute | solution.py:496
  11.8 10.0 %collective-permute-start.31 = (bf16[16,2048]{1,0:T(8,128)(2,1)S(1)}, bf16[16,2048]{1,0:T(8,128)(2,1)S(1)}, u32[]{:S(2)}, u32[]{:S(2)}) collective-permute-start(bf16[16,2048]{1,0:T(8,128)(2,1)S(1)} %get-tuple-element.228), channel_id=1, source_target_pairs={{0,8},{4,12},{8,0},{12,4},{1,9},{5,13},{9,1},{13,5},{2,10},{6,14},... | collective-permute-start | bytes 196616 | tf_op jit(solution)/shard_map/ppermute | solution.py:496
  18.2 4.3 %collective-permute-start.32 = (bf16[16,2048]{1,0:T(8,128)(2,1)S(1)}, bf16[16,2048]{1,0:T(8,128)(2,1)S(1)}, u32[]{:S(2)}, u32[]{:S(2)}) collective-permute-start(bf16[16,2048]{1,0:T(8,128)(2,1)S(1)} %get-tuple-element.229), channel_id=1, source_target_pairs={{0,12},{4,0},{8,4},{12,8},{1,13},{5,1},{9,5},{13,9},{2,14},{6,2},{... | collective-permute-start | bytes 196616 | tf_op jit(solution)/shard_map/ppermute | solution.py:496
  22.5 6.6 %collective-permute-start.34 = (bf16[64,2048]{1,0:T(8,128)(2,1)S(1)}, bf16[64,2048]{1,0:T(8,128)(2,1)S(1)}, u32[]{:S(2)}, u32[]{:S(2)}) collective-permute-start(bf16[64,2048]{1,0:T(8,128)(2,1)S(1)} %constant_dynamic-update-slice_fusion.refs_0_), channel_id=1, source_target_pairs={{0,2},{1,3},{2,0},{3,1},{4,6},{5,7},{6,4},{7,5},{8,10},{9,11},{10,... | collective-permute-start | bytes 786440 | tf_op jit(solution)/shard_map/ppermute | solution.py:492
  24.0 5.2 %collective-permute-start.33 = (bf16[64,2048]{1,0:T(8,128)(2,1)S(1)}, bf16[64,2048]{1,0:T(8,128)(2,1)S(1)}, u32[]{:S(2)}, u32[]{:S(2)}) collective-permute-start(bf16[64,2048]{1,0:T(8,128)(2,1)S(1)} %constant_dynamic-update-slice_fusion.refs_0_), channel_id=1, source_target_pairs={{0,1},{1,0},{2,3},{3,2},{4,5},{5,4},{6,7},{7,6},{8,9},{9,8},{10,11... | collective-permute-start | bytes 786440 | tf_op jit(solution)/shard_map/ppermute | solution.py:492
  29.1 1.5 %collective-permute-start.35 = (bf16[64,2048]{1,0:T(8,128)(2,1)S(1)}, bf16[64,2048]{1,0:T(8,128)(2,1)S(1)}, u32[]{:S(2)}, u32[]{:S(2)}) collective-permute-start(bf16[64,2048]{1,0:T(8,128)(2,1)S(1)} %collective-permute-done.34.refs_2_), channel_id=1, source_target_pairs={{0,1},{1,0},{2,3},{3,2},{4,5},{5,4},{6,7},{7,6},{8,9},{9,8},{10,11... | collective-permute-start | bytes 786440 | tf_op jit(solution)/shard_map/ppermute | solution.py:492
  36.5 9.1 %collective-permute-start.12 = (bf16[144,1024]{1,0:T(8,128)(2,1)S(1)}, bf16[144,1024]{1,0:T(8,128)(2,1)S(1)}, u32[]{:S(2)}, u32[]{:S(2)}) collective-permute-start(bf16[144,1024]{1,0:T(8,128)(2,1)S(1)} %get-tuple-element.132), channel_id=1, source_target_pairs={{0,4},{4,0},{8,12},{12,8},{1,5},{5,1},{9,13},{13,9},{2,6},{6,2},{1... | collective-permute-start | bytes 884744 | tf_op jit(solution)/shard_map/cond/branch_2_fun/ppermute | solution.py:492
  45.7 14.6 %collective-permute-start.13 = (bf16[144,1024]{1,0:T(8,128)(2,1)S(1)}, bf16[144,1024]{1,0:T(8,128)(2,1)S(1)}, u32[]{:S(2)}, u32[]{:S(2)}) collective-permute-start(bf16[144,1024]{1,0:T(8,128)(2,1)S(1)} %get-tuple-element.136), channel_id=1, source_target_pairs={{0,4},{4,0},{8,12},{12,8},{1,5},{5,1},{9,13},{13,9},{2,6},{6,2},{1... | collective-permute-start | bytes 884744 | tf_op jit(solution)/shard_map/cond/branch_2_fun/ppermute | solution.py:492
  46.4 13.9 %collective-permute-start.14 = (bf16[144,1024]{1,0:T(8,128)(2,1)S(1)}, bf16[144,1024]{1,0:T(8,128)(2,1)S(1)}, u32[]{:S(2)}, u32[]{:S(2)}) collective-permute-start(bf16[144,1024]{1,0:T(8,128)(2,1)S(1)} %add_convert_fusion.2), channel_id=1, source_target_pairs={{0,8},{4,12},{8,0},{12,4},{1,9},{5,13},{9,1},{13,5},{2,10},{6,14},... | collective-permute-start | bytes 884744 | tf_op jit(solution)/shard_map/cond/branch_2_fun/ppermute | solution.py:492
  60.4 12.4 %collective-permute-start.16 = (bf16[144,1024]{1,0:T(8,128)(2,1)S(1)}, bf16[144,1024]{1,0:T(8,128)(2,1)S(1)}, u32[]{:S(2)}, u32[]{:S(2)}) collective-permute-start(bf16[144,1024]{1,0:T(8,128)(2,1)S(1)} %multiply_convert_fusion.2.refs_0_), channel_id=1, source_target_pairs={{0,4},{4,0},{8,12},{12,8},{1,5},{5,1},{9,13},{13,9},{2,6},{6,2},{1... | collective-permute-start | bytes 884744 | tf_op jit(solution)/shard_map/cond/branch_2_fun/ppermute | solution.py:492
  62.5 14.6 %collective-permute-start.15 = (bf16[144,1024]{1,0:T(8,128)(2,1)S(1)}, bf16[144,1024]{1,0:T(8,128)(2,1)S(1)}, u32[]{:S(2)}, u32[]{:S(2)}) collective-permute-start(bf16[144,1024]{1,0:T(8,128)(2,1)S(1)} %multiply_convert_fusion.2.refs_0_), channel_id=1, source_target_pairs={{0,8},{4,12},{8,0},{12,4},{1,9},{5,13},{9,1},{13,5},{2,10},{6,14},... | collective-permute-start | bytes 884744 | tf_op jit(solution)/shard_map/cond/branch_2_fun/ppermute | solution.py:492
  77.2 7.5 %collective-permute-start.17 = (bf16[144,1024]{1,0:T(8,128)(2,1)S(1)}, bf16[144,1024]{1,0:T(8,128)(2,1)S(1)}, u32[]{:S(2)}, u32[]{:S(2)}) collective-permute-start(bf16[144,1024]{1,0:T(8,128)(2,1)S(1)} %collective-permute-done.15.refs_0_), channel_id=1, source_target_pairs={{0,4},{4,0},{8,12},{12,8},{1,5},{5,1},{9,13},{13,9},{2,6},{6,2},{1... | collective-permute-start | bytes 884744 | tf_op jit(solution)/shard_map/cond/branch_2_fun/ppermute | solution.py:492
  87.8 1.8 %collective-permute-start.36 = (bf16[384,512]{1,0:T(8,128)(2,1)S(1)}, bf16[384,512]{1,0:T(8,128)(2,1)S(1)}, u32[]{:S(2)}, u32[]{:S(2)}) collective-permute-start(bf16[384,512]{1,0:T(8,128)(2,1)S(1)} %get-tuple-element.233), channel_id=1, source_target_pairs={{0,1},{1,0},{2,3},{3,2},{4,5},{5,4},{6,7},{7,6},{8,9},{9,8},{10,11... | collective-permute-start | bytes 1179656 | tf_op jit(solution)/shard_map/ppermute | solution.py:492
  89.6 7.0 %collective-permute-start.37 = (bf16[192,512]{1,0:T(8,128)(2,1)S(1)}, bf16[192,512]{1,0:T(8,128)(2,1)S(1)}, u32[]{:S(2)}, u32[]{:S(2)}) collective-permute-start(bf16[192,512]{1,0:T(8,128)(2,1)S(1)} %add_convert_fusion.6), channel_id=1, source_target_pairs={{0,2},{1,3},{2,0},{3,1},{4,6},{5,7},{6,4},{7,5},{8,10},{9,11},{10,... | collective-permute-start | bytes 589832 | tf_op jit(solution)/shard_map/ppermute | solution.py:492
  96.7 4.7 %collective-permute-start.38 = (bf16[48,512]{1,0:T(8,128)(2,1)S(1)}, bf16[48,512]{1,0:T(8,128)(2,1)S(1)}, u32[]{:S(2)}, u32[]{:S(2)}) collective-permute-start(bf16[48,512]{1,0:T(8,128)(2,1)S(1)} %get-tuple-element.236), channel_id=1, source_target_pairs={{0,12},{4,0},{8,4},{12,8},{1,13},{5,1},{9,5},{13,9},{2,14},{6,2},{... | collective-permute-start | bytes 147464 | tf_op jit(solution)/shard_map/ppermute | solution.py:496
  99.7 5.0 %collective-permute-start.39 = (bf16[48,512]{1,0:T(8,128)(2,1)S(1)}, bf16[48,512]{1,0:T(8,128)(2,1)S(1)}, u32[]{:S(2)}, u32[]{:S(2)}) collective-permute-start(bf16[48,512]{1,0:T(8,128)(2,1)S(1)} %get-tuple-element.235), channel_id=1, source_target_pairs={{0,8},{4,12},{8,0},{12,4},{1,9},{5,13},{9,1},{13,5},{2,10},{6,14},... | collective-permute-start | bytes 147464 | tf_op jit(solution)/shard_map/ppermute | solution.py:496
  99.7 5.9 %collective-permute-start.40 = (bf16[48,512]{1,0:T(8,128)(2,1)S(1)}, bf16[48,512]{1,0:T(8,128)(2,1)S(1)}, u32[]{:S(2)}, u32[]{:S(2)}) collective-permute-start(bf16[48,512]{1,0:T(8,128)(2,1)S(1)} %get-tuple-element.234), channel_id=1, source_target_pairs={{0,4},{4,8},{8,12},{12,0},{1,5},{5,9},{9,13},{13,1},{2,6},{6,10},{... | collective-permute-start | bytes 147464 | tf_op jit(solution)/shard_map/ppermute | solution.py:496
